TPU v7x, 32 devices: a whole 2x2x4 slice. The times are simulated.
32 devices in a mesh: dp: 8 (over z, y), tensor: 4 (over x, core).
Axes of the slice: x: 2, y: 2, z: 4, core: 2. Of those that a mesh axis runs over, the one named last changes fastest.
Arguments:
- tokens: bfloat16 [8, 512, 2048], P('dp', 'tensor'), may hold values from -6 to 6
- cotangent: bfloat16 [8, 512, 2048], P('dp', 'tensor'), may hold values from -6 to 6
- block_ids: int32 [8, 512], P('dp'), may hold values from 0 to 3, never falling along the last dimension, each value on 1 to 256 neighbouring positions
- w_qkv: float32 [3, 2048, 2048], P(None, 'dp', 'tensor'), may hold values from -0.110485435 to 0.110485435
- m_qkv: float32 [3, 2048, 2048], P(None, 'dp', 'tensor'), may hold values from -40 to 40
- v_qkv: float32 [3, 2048, 2048], P(None, 'dp', 'tensor'), may hold values from 204.8 to 819.2
- w_out: float32 [2048, 2048], P('tensor', 'dp'), may hold values from -0.125 to 0.125
- m_out: float32 [2048, 2048], P('tensor', 'dp'), may hold values from -40 to 40
- v_out: float32 [2048, 2048], P('tensor', 'dp'), may hold values from 204.8 to 819.2
- w_gu: float32 [2, 2048, 8192], P(None, 'dp', 'tensor'), may hold values from -0.125 to 0.125
- m_gu: float32 [2, 2048, 8192], P(None, 'dp', 'tensor'), may hold values from -40 to 40
- v_gu: float32 [2, 2048, 8192], P(None, 'dp', 'tensor'), may hold values from 204.8 to 819.2
- w_down: float32 [8192, 2048], P('tensor', 'dp'), may hold values from -0.0625 to 0.0625
- m_down: float32 [8192, 2048], P('tensor', 'dp'), may hold values from -40 to 40
- v_down: float32 [8192, 2048], P('tensor', 'dp'), may hold values from 204.8 to 819.2
- gains: float32 [4, 2048], P(None, 'dp'), may hold values from 0.7 to 1.6
- gain_m: float32 [4, 2048], P(None, 'dp'), may hold values from -40 to 40
- gain_v: float32 [4, 2048], P(None, 'dp'), may hold values from 204.8 to 819.2
Outputs:
- output: bfloat16 [8, 512, 2048], P('dp', 'tensor')
- grad_tokens: float32 [8, 512, 2048], P('dp', 'tensor')
- new_w_qkv: float32 [3, 2048, 2048], P(None, 'dp', 'tensor')
- new_m_qkv: float32 [3, 2048, 2048], P(None, 'dp', 'tensor')
- new_v_qkv: float32 [3, 2048, 2048], P(None, 'dp', 'tensor')
- copy_qkv: bfloat16 [3, 2048, 2048], P(None, 'dp', 'tensor')
- new_w_out: float32 [2048, 2048], P('tensor', 'dp')
- new_m_out: float32 [2048, 2048], P('tensor', 'dp')
- new_v_out: float32 [2048, 2048], P('tensor', 'dp')
- copy_out: bfloat16 [2048, 2048], P('tensor', 'dp')
- new_w_gu: float32 [2, 2048, 8192], P(None, 'dp', 'tensor')
- new_m_gu: float32 [2, 2048, 8192], P(None, 'dp', 'tensor')
- new_v_gu: float32 [2, 2048, 8192], P(None, 'dp', 'tensor')
- copy_gu: bfloat16 [2, 2048, 8192], P(None, 'dp', 'tensor')
- new_w_down: float32 [8192, 2048], P('tensor', 'dp')
- new_m_down: float32 [8192, 2048], P('tensor', 'dp')
- new_v_down: float32 [8192, 2048], P('tensor', 'dp')
- copy_down: bfloat16 [8192, 2048], P('tensor', 'dp')
- new_gains: float32 [4, 2048], P(None, 'dp')
- new_gain_m: float32 [4, 2048], P(None, 'dp')
- new_gain_v: float32 [4, 2048], P(None, 'dp')
- clip_factor: float32 [16], P('tensor')
Inputs may be any that keep to these rules, and one draw needn't show every extreme that they name: `block_ids`: along a row block numbers never fall; every block holds 1 to 256 positions and some block holds exactly 256.
All inputs are finite; a program needn't handle non-finite values.
Results may differ from a plain program's by a relative error of at most 0.025.
Values may be sent and summed in bfloat16 or wider, within the bound.
A program may use at most 192 MiB of HBM per device.

v0:
```python
import jax
import jax.numpy as jnp
import numpy as np
from jax import lax
from jax.experimental import pallas as pl
from jax.experimental.pallas import tpu as pltpu
from jax.sharding import PartitionSpec as P

HEAD = 128
STEP = 5


norm_eps = 1e-06
rope_base = 500000.0
beta_one = 0.9
beta_two = 0.95
rate_matrix = 0.01
rate_gain = 0.6
weight_decay = 0.1
adam_eps = 1e-08
clip_tau = 9.0
masked_value = -1e30


def rope_tables(length, size):
    half = size // 2
    freq = np.float32(rope_base) ** (-(np.arange(half, dtype=np.float32) * np.float32(2.0 / size)))
    angle = np.arange(length, dtype=np.float32)[:, None] * freq[None, :]
    angle = np.concatenate([angle, angle], axis=1)
    return (jnp.asarray(np.cos(angle)), jnp.asarray(np.sin(angle)))


def adam_step(param, grad, first, second, rate, decay):
    first = beta_one * first + (1.0 - beta_one) * grad
    second = beta_two * second + (1.0 - beta_two) * grad * grad
    fix_one = 1.0 - beta_one**STEP
    fix_two = 1.0 - beta_two**STEP
    update = first / fix_one / (jnp.sqrt(second / fix_two) + adam_eps)
    return (param - rate * (update + decay * param), first, second)


class Grid:
    def __init__(self):
        self.dp = lax.axis_size("dp")
        self.tensor = lax.axis_size("tensor")
        self.inner = 1
        while self.inner * self.inner * 4 <= self.dp:
            self.inner *= 2
        self.outer = self.dp // self.inner
        self.chips = self.tensor // 2
        self.dp_at = lax.axis_index("dp")
        self.tensor_at = lax.axis_index("tensor")
        self.inner_at = self.dp_at % self.inner
        self.chip_at = self.tensor_at // 2
        self.core_at = self.tensor_at % 2
        self.outer_at = self.dp_at // self.inner

    def path_of(self, index):
        column, row = index // self.inner, index % self.inner
        return row * self.outer + column + (row % 2) * (self.outer - 1 - 2 * column)

    def outer_flip(self, index, step):
        result = 0
        for bit in bits(self.outer):
            side = index // bit % 2
            result = result + bit * (1 - side if step & bit else side)
        return result

    def index_of(self, place):
        row, column = place // self.outer, place % self.outer
        return (column + (row % 2) * (self.outer - 1 - 2 * column)) * self.inner + row


def bits(count):
    return [1 << k for k in range(count.bit_length() - 1)]


def greet(peers):
    barrier = pltpu.get_barrier_semaphore()
    for peer in peers:
        pl.semaphore_signal(barrier, inc=1, device_id=peer, device_id_type=pl.DeviceIdType.MESH)
    pl.semaphore_wait(barrier, len(peers))


def attend_back_call(
    d_resid, attn_hat, o_scale, gain_rows, full_out, context, q_low, k_low, v_low, lse, hats, scales,
    tables, blocks, seq, full_qkv, gain_last, tops, unit_grads,
):
    grid = Grid()
    n, outer, inner, chips, tensor = grid.dp, grid.outer, grid.inner, grid.chips, grid.tensor
    count, width = d_resid.shape
    length, span = context.shape
    heads = span // HEAD
    slab, units = unit_grads[0][0].shape[1:]
    thin = width // n
    half = span // 2
    tall = min(256, length)
    tile = 512
    lines = 32
    ring = 8 + 2
    gain_item, top_item = 8, 9
    bf16, f32 = jnp.bfloat16, jnp.float32
    mesh_id = pl.DeviceIdType.MESH
    flat_grads = [unit_grads[c][j] for j in range(inner) for c in range(3)]
    some = len(flat_grads)
    z_steps = list(range(1, outer))

    def kernel(*refs):
        fixed, far_in, grads_in = refs[:17], refs[17:20], refs[20 : 20 + some]
        rest = refs[20 + some :]
        body(*fixed, far_in, grads_in, *rest)

    def body(
        dres_ref, hat_ref, o_scale_ref, gain_ref, out_w, ctx, q_ref, k_ref, v_ref, lse_ref, scale_ref,
        cos_ref, sin_ref, id_col, id_row, last_ref, tops_ref, far_in, grads_in,
        gu_out, down_out, part_ref, part_out, gains_out, tops_out, tokens_out,
        hats, seq, qkv_w, seq_do, d_ctx, d_q, d_k, d_v, d_low, probs_low, whole, terms, row_terms, turned,
        land, land_gain, land_top, own_gain, peer_gain, inners, peer_inners,
        gu_land, gu_sum, down_land, down_sum, core_send, core_land, hold, chip_send, chip_land,
        s_ring, r_ring, s_row, r_row, s_in, r_in, s_y, r_y, s_z, r_z, s_core, r_core, s_chip, r_chip, s_gain, r_gain, local,
    ):
        hats_in, seq_in, qkv_in = far_in
        g = Grid()

        def tensor_peer(k, flip):
            core = 1 - g.core_at if flip else g.core_at
            return (g.dp_at, lax.rem(g.chip_at + k + chips, chips) * 2 + core)

        def dp_peer(s, j):
            across = g.outer_flip(g.outer_at, s) * inner
            return (across + lax.rem(g.inner_at + j + inner, inner), g.tensor_at)

        place = g.path_of(g.dp_at)
        after_dp = (g.index_of(lax.rem(place + 1, n)), g.tensor_at)
        before_dp = (g.index_of(lax.rem(place + n - 1, n)), g.tensor_at)
        near = [tensor_peer(k, f) for k in range(chips) for f in (0, 1) if (k, f) != (0, 0)]
        far = [dp_peer(s, 0) for s in range(1, outer)] + [dp_peer(0, j) for j in range(1, inner)]
        greet(near + far + [after_dp, before_dp])

        def remote(src, dst, send, recv, peer):
            copy = pltpu.make_async_remote_copy(
                src_ref=src, dst_ref=dst, send_sem=send, recv_sem=recv,
                device_id=peer, device_id_type=mesh_id,
            )
            copy.start()
            return copy

        def fetch(src, dst, at):
            copy = pltpu.make_async_copy(src, dst, local.at[at])
            copy.start()
            return copy

        def dot(a, b, contract):
            return lax.dot_general(a, b, (contract, ((), ())), preferred_element_type=f32)

        def looped(total, make):
            lax.fori_loop(0, total, lambda i, c: (make(i), c)[1], 0, unroll=total <= 4)

        def rows_of(i, size):
            return pl.ds(pl.multiple_of(i * size, size), size)

        sent = []
        y_copies = {}
        sum_steps = [(c, s) for c in range(3) for s in z_steps + [0]]
        for c, s in sum_steps:
            for j in range(1, inner):
                copy = remote(
                    grads_in[j * 3 + c].at[s],
                    down_land.at[j - 1, s] if c == 2 else gu_land.at[j - 1, c, s],
                    s_y.at[j, c, s],
                    r_y.at[j, c, s],
                    dp_peer(0, j),
                )
                y_copies[j, c, s] = copy
                sent.append(copy)
        own_refs = (gu_sum.at[0], gu_sum.at[1], down_sum)
        own_grads = [fetch(grads_in[c], own_refs[c], c) for c in range(3)]
        fetched = [fetch(hats_in, hats, 3), fetch(seq_in, seq, 4), fetch(qkv_in, qkv_w, 5)]
        z_copies = []
        keeps = []

        def unit_sums(times):
            for _ in range(times):
                if sum_steps:
                    unit_sum(*sum_steps.pop(0))

        def unit_sum(c, s):
            if s == (z_steps + [0])[0]:
                own_grads[c].wait()
            for j in range(1, inner):
                y_copies[j, c, s].wait_recv()

            def add_gu(i):
                rows = rows_of(i, 64)
                total = gu_sum[c, s, rows].astype(f32)
                for j in range(1, inner):
                    total = total + gu_land[j - 1, c, s, rows].astype(f32)
                gu_sum[c, s, rows] = total.astype(bf16)

            def add_down(i):
                rows = rows_of(i, 64)
                total = down_sum[s, rows].astype(f32)
                for j in range(1, inner):
                    total = total + down_land[j - 1, s, rows].astype(f32)
                down_sum[s, rows] = total.astype(bf16)

            there = rows_of(g.outer_at, units)
            if c == 2:
                looped(units // 64, add_down)
                src, dst = down_sum.at[s], down_out.at[there]
            else:
                looped(slab // 64, add_gu)
                src, dst = gu_sum.at[c, s], gu_out.at[c, :, there]
            if s:
                z_copies.append(remote(src, dst, s_z.at[c, s], r_z.at[c, s], dp_peer(s, 0)))
            else:
                keeps.append(fetch(src, dst, 6 + c))

        def way_of(item):
            return 1 if item >= 8 else 1 - 2 * (item // 4)

        def own(item, away):
            index = g.index_of(lax.rem(place - way_of(item) * away + 2 * n, n))
            if item == gain_item:
                return terms.at[index]
            if item == top_item:
                return tops_ref
            side, c = item // 4, item % 4
            return whole.at[c, pl.ds(side * half, half), rows_of(index, thin)]

        def landed(step, item):
            if item == gain_item:
                return land_gain.at[step]
            if item == top_item:
                return land_top.at[step]
            return land.at[step, item]

        hops = {}
        on_path = {}

        def hop(step, item):
            hops[step, item] = remote(
                own(item, 1) if step == 0 else landed(step - 1, item),
                landed(step, item),
                s_ring.at[step, item],
                r_ring.at[step, item],
                after_dp if way_of(item) == 1 else before_dp,
            )

        def depart(*items):
            for item in items:
                on_path[item] = 0
                hop(0, item)

        def advance(*items):
            for item in items:
                step = on_path.get(item, n) + 1
                if step >= n:
                    continue
                on_path[item] = step
                hops[step - 1, item].wait_recv()
                here = landed(step - 1, item)
                if item == top_item:
                    summed = jnp.maximum(here[...], tops_ref[...])
                else:
                    summed = here[...].astype(f32) + own(item, step + 1)[...].astype(f32)
                if step < n - 1:
                    here[...] = summed.astype(here.dtype)
                    hop(step, item)
                elif item == gain_item:
                    own_gain[0] = summed
                elif item == top_item:
                    tops_out[...] = summed
                else:
                    side, c = item // 4, item % 4
                    span_half = pl.ds(side * half, half)
                    if c == 3:
                        part_out[span_half] = summed
                    else:
                        part_ref[c, :, span_half] = summed.T

        def matrix_grad(c, left, right):
            turned[...] = left.T

            def columns(i):
                cols = rows_of(i, tile)
                whole[c, :, cols] = dot(turned[...], right[:, cols], ((1,), (0,))).astype(bf16)

            looped(width // tile, columns)

        t_at = g.tensor_at
        mine = rows_of(t_at, count)

        def open_rows(i, total):
            at = rows_of(i, lines)
            value, hat = dres_ref[at], hat_ref[at]
            upstream = value * gain_ref[2:3]
            mean = jnp.mean(upstream * hat, axis=1, keepdims=True)
            d_attn = (o_scale_ref[at] * (upstream - hat * mean)).astype(bf16)
            seq_do[pl.ds(pl.multiple_of(t_at * count + i * lines, lines), lines)] = d_attn
            return total + jnp.sum(value * hat, axis=0, keepdims=True)

        gain_attn = lax.fori_loop(0, count // lines, open_rows, jnp.zeros((1, width), f32))
        row_terms[...] = jnp.zeros((8, width), f32)
        row_terms[2:3] = gain_attn
        row_terms[3:4] = last_ref[...]
        moves, passed = [], []

        def row_copy(slot, index, peer):
            at = rows_of(index, count)
            copy = remote(seq_do.at[at], seq_do.at[at], s_row.at[slot], r_row.at[slot], peer)
            sent.append(copy)
            return copy

        for k in range(1, chips):
            moves.append(row_copy(k - 1, t_at, tensor_peer(k, 0)))
        to_core = row_copy(chips - 1, t_at, tensor_peer(0, 1))
        unit_sums(1)
        scale = HEAD ** (-0.5)
        for h in range(heads):
            cols = slice(h * HEAD, (h + 1) * HEAD)

            def weigh(i, c, cols=cols, h=h):
                at = rows_of(i, tall)
                raw = dot(q_ref[at, cols], k_ref[:, cols], ((1,), (1,))) * scale
                masked = jnp.where(id_row[...] <= id_col[at], raw, masked_value)
                probs_low[h, at] = jnp.exp(masked - lse_ref[at, h : h + 1]).astype(bf16)
                return c

            lax.fori_loop(0, length // tall, weigh, 0, unroll=length // tall <= 4)
            if 2 * (h + 1) == heads:
                unit_sums(1)
        for k in range(1, chips):
            moves[k - 1].wait_recv()
            source = lax.rem(g.chip_at - k + chips, chips) * 2 + g.core_at
            passed.append(row_copy(chips - 1 + k, source, tensor_peer(0, 1)))
        to_core.wait_recv()
        unit_sums(1)
        for copy in passed:
            copy.wait_recv()

        def context_grad(i):
            at = rows_of(i, tall)
            d_ctx[at] = dot(seq_do[at], out_w[...], ((1,), (1,))).astype(bf16)

        looped(length // tall, context_grad)
        unit_sums(1)

        for h in range(heads):
            cols = slice(h * HEAD, (h + 1) * HEAD)

            def head(i, c, cols=cols, h=h):
                at = rows_of(i, tall)
                q_part, ctx_part = q_ref[at, cols], d_ctx[at, cols]
                probs_part = probs_low[h, at]
                probs = probs_part.astype(f32)
                d_probs = dot(ctx_part, v_ref[:, cols], ((1,), (1,)))
                mean = jnp.sum(probs * d_probs, axis=1, keepdims=True)
                d_scores = (probs * (d_probs - mean)).astype(bf16)
                d_q[at, cols] = dot(d_scores, k_ref[:, cols], ((1,), (0,))) * scale
                key = dot(d_scores, q_part, ((0,), (0,))) * scale
                value = dot(probs_part, ctx_part, ((0,), (0,)))
                d_k[:, cols] = jnp.where(i == 0, key, d_k[:, cols] + key)
                d_v[:, cols] = jnp.where(i == 0, value, d_v[:, cols] + value)
                return c

            d_k[:, cols] = jnp.zeros((length, HEAD), f32)
            d_v[:, cols] = jnp.zeros((length, HEAD), f32)
            lax.fori_loop(0, length // tall, head, 0, unroll=length // tall <= 4)
            unit_sums(1)
        fetched[0].wait()
        sign = jnp.where(lax.broadcasted_iota(jnp.int32, (tall, HEAD), 1) < HEAD // 2, -1.0, 1.0)

        def unrotate(i, sums):
            at = rows_of(i, tall)
            cosine, sine = cos_ref[at], sin_ref[at]
            lane = lax.broadcasted_iota(jnp.int32, (tall, 128), 1)
            columns = jnp.zeros((tall, 128), f32)
            result = []
            for c, grad in ((0, d_q), (1, d_k)):
                total = jnp.zeros((tall, 1), f32)
                terms_row = []
                for h in range(heads):
                    cols = slice(h * HEAD, (h + 1) * HEAD)
                    value = grad[at, cols]
                    back = value * cosine - pltpu.roll(value * sine, HEAD // 2, 1) * sign
                    hat = hats[c, at, cols]
                    terms_row.append(jnp.sum(back * hat, axis=0, keepdims=True))
                    at_head = pl.ds(pl.multiple_of(t_at * span + h * HEAD, HEAD), HEAD)
                    back = back * gain_ref[c : c + 1, at_head]
                    grad[at, cols] = back
                    total = total + jnp.sum(back * hat, axis=1, keepdims=True)
                columns = jnp.where(lane == c, total, columns)
                result.append(sums[c] + jnp.concatenate(terms_row, axis=1))
            inners[:, at] = columns.T[:8]
            return tuple(result)

        zero = jnp.zeros((1, span), f32)
        gain_q, gain_k = lax.fori_loop(0, length // tall, unrotate, (zero, zero))
        offset = rows_of(t_at, span)
        row_terms[0:1, offset] = gain_q
        row_terms[1:2, offset] = gain_k
        in_copies = []
        for k in range(chips):
            for f in (0, 1):
                if (k, f) != (0, 0):
                    at = k * 2 + f - 1
                    in_copies.append(
                        remote(inners, peer_inners.at[at], s_in.at[at], r_in.at[at], tensor_peer(k, f))
                    )
        sent.extend(in_copies)
        matrix_grad(3, ctx[...], seq_do)
        depart(3, 7)
        for copy in in_copies:
            copy.wait_recv()
        unit_sums(1)

        def normed(i):
            at = rows_of(i, tall)
            sums = inners[:, at]
            for other in range(tensor - 1):
                sums = sums + peer_inners[other, :, at]
            column = jnp.concatenate([sums, jnp.zeros((120, tall), f32)], axis=0).T / width
            for c, grad in ((0, d_q), (1, d_k)):
                value = grad[at] - hats[c, at] * column[:, c : c + 1]
                d_low[c, at] = (scale_ref[at, c : c + 1] * value).astype(bf16)
            d_low[2, at] = d_v[at].astype(bf16)

        looped(length // tall, normed)
        fetched[1].wait()
        for c in (2, 0, 1):
            matrix_grad(c, d_low[c], seq)
            depart(c, c + 4)
            unit_sums(1)

        def place_terms(i, c):
            cols = pl.ds(pl.multiple_of(i * thin, thin), thin)
            terms[i] = row_terms[:, cols]
            return c

        lax.fori_loop(0, n, place_terms, 0)

        depart(gain_item, top_item)
        unit_sums(len(sum_steps))

        fetched[2].wait()
        chip_order = list(range(1, chips)) + [0]
        core_copies, chip_copies = {}, {}

        def token_rows(k, flip, store):
            chip = lax.rem(g.chip_at + k, chips)
            core = 1 - g.core_at if flip else g.core_at
            at = rows_of(chip * 2 + core, count)

            def columns(i):
                cols = rows_of(i, tile)
                total = dot(d_low[0, at], qkv_w[0, cols], ((1,), (1,)))
                for c in (1, 2):
                    total = total + dot(d_low[c, at], qkv_w[c, cols], ((1,), (1,)))
                store(cols, total)

            looped(width // tile, columns)

        duties = []
        for k in chip_order:

            def away(k=k):
                def store(cols, value):
                    core_send[k, :, cols] = value.astype(bf16)

                token_rows(k, True, store)
                core_copies[k] = remote(
                    core_send.at[k], core_land.at[k], s_core.at[k], r_core.at[k], tensor_peer(0, 1)
                )

            def here(k=k):
                def store(cols, value):
                    hold[k, :, cols] = value

                token_rows(k, False, store)

            def join(k=k):
                core_copies[k].wait_recv()

                def add(i):
                    at = rows_of(i, lines)
                    chip_send[k - 1, at] = (hold[k, at] + core_land[k, at].astype(f32)).astype(bf16)

                looped(count // lines, add)
                chip_copies[k] = remote(
                    chip_send.at[k - 1], chip_land.at[k - 1], s_chip.at[k], r_chip.at[k], tensor_peer(k, 0)
                )

            duties += [away, here] + ([join] if k else [])

        def close_tokens():
            core_copies[0].wait_recv()
            for k in range(1, chips):
                chip_copies[k].wait_recv()

            def close(i):
                at = rows_of(i, lines)
                total = dres_ref[at] + hold[0, at] + core_land[0, at].astype(f32)
                for k in range(1, chips):
                    total = total + chip_land[k - 1, at].astype(f32)
                tokens_out[at] = total

            looped(count // lines, close)

        duties.append(close_tokens)
        per_step = -(-len(duties) // (n - 2))
        for step in range(1, n):
            advance(3, 7, 2, 6, 0, 4, 1, 5, gain_item, top_item)
            for _ in range(per_step):
                if duties:
                    duties.pop(0)()
        peers = [tensor_peer(0, 1)] + [tensor_peer(k, 0) for k in range(1, chips)]
        first = remote(own_gain.at[0], peer_gain.at[0], s_gain.at[0], r_gain.at[0], peers[0])
        first.wait_recv()
        own_gain[1] = own_gain[0] + peer_gain[0]
        others = [
            remote(own_gain.at[1], peer_gain.at[k], s_gain.at[k], r_gain.at[k], peers[k])
            for k in range(1, chips)
        ]
        result = own_gain[1]
        for k in range(1, chips):
            others[k - 1].wait_recv()
            result = result + peer_gain[k]
        gains_out[...] = result
        for copy in z_copies:
            copy.wait()
        for copy in keeps:
            copy.wait()
        for copy in sent + list(hops.values()) + list(core_copies.values()):
            copy.wait_send()
        for copy in list(chip_copies.values()) + [first] + others:
            copy.wait_send()

    shape = jax.ShapeDtypeStruct
    anywhere = pl.BlockSpec(memory_space=pl.ANY)
    vmem = pl.BlockSpec(memory_space=pltpu.VMEM)
    sems = pltpu.SemaphoreType.DMA
    results = pl.pallas_call(
        kernel,
        out_shape=(
            shape((2, slab, outer * units), bf16),
            shape((outer * units, slab), bf16),
            shape((3, thin, span), f32),
            shape((span, thin), f32),
            shape((8, thin), f32),
            shape(tops.shape, f32),
            shape((count, width), f32),
        ),
        in_specs=[vmem] * 17 + [anywhere] * 3 + [anywhere] * some,
        out_specs=(anywhere,) * 2 + (vmem,) * 5,
        scratch_shapes=[
            pltpu.VMEM(hats.shape, f32),
            pltpu.VMEM(seq.shape, bf16),
            pltpu.VMEM(full_qkv.shape, bf16),
            pltpu.VMEM((length, width), bf16),
            pltpu.VMEM((length, span), bf16),
            pltpu.VMEM((length, span), f32),
            pltpu.VMEM((length, span), f32),
            pltpu.VMEM((length, span), f32),
            pltpu.VMEM((3, length, span), bf16),
            pltpu.VMEM((heads, length, length), bf16),
            pltpu.VMEM((4, span, width), bf16),
            pltpu.VMEM((n, 8, thin), f32),
            pltpu.VMEM((8, width), f32),
            pltpu.VMEM((span, length), bf16),
            pltpu.VMEM((n - 1, 8, half, thin), bf16),
            pltpu.VMEM((n - 1, 8, thin), f32),
            pltpu.VMEM((n - 1,) + tops.shape, f32),
            pltpu.VMEM((2, 8, thin), f32),
            pltpu.VMEM((chips, 8, thin), f32),
            pltpu.VMEM((8, length), f32),
            pltpu.VMEM((tensor - 1, 8, length), f32),
            pltpu.VMEM((max(inner - 1, 1), 2, outer, slab, units), bf16),
            pltpu.VMEM((2, outer, slab, units), bf16),
            pltpu.VMEM((max(inner - 1, 1), outer, units, slab), bf16),
            pltpu.VMEM((outer, units, slab), bf16),
            pltpu.VMEM((chips, count, width), bf16),
            pltpu.VMEM((chips, count, width), bf16),
            pltpu.VMEM((chips, count, width), f32),
            pltpu.VMEM((max(chips - 1, 1), count, width), bf16),
            pltpu.VMEM((max(chips - 1, 1), count, width), bf16),
            sems((n - 1, ring)),
            sems((n - 1, ring)),
            sems((2 * chips - 1,)),
            sems((2 * chips - 1,)),
            sems((tensor - 1,)),
            sems((tensor - 1,)),
            sems((inner, 3, outer)),
            sems((inner, 3, outer)),
            sems((3, outer)),
            sems((3, outer)),
            sems((chips,)),
            sems((chips,)),
            sems((chips,)),
            sems((chips,)),
            sems((chips,)),
            sems((chips,)),
            sems((9,)),
        ],
        compiler_params=pltpu.CompilerParams(
            collective_id=1, has_side_effects=True, vmem_limit_bytes=61 * 2**20
        ),
    )(
        d_resid, attn_hat, o_scale, gain_rows, full_out, context, q_low, k_low, v_low, lse, scales,
        tables[0], tables[1], blocks[:, None], blocks[None, :], gain_last, tops,
        hats, seq, full_qkv, *flat_grads,
    )
    return results


def open_call(w_qkv, w_out, gains, rows, w_gu, w_down, tables, blocks):
    grid = Grid()
    n, outer, inner = grid.dp, grid.outer, grid.inner
    chips, tensor = grid.chips, grid.tensor
    count, width = rows.shape
    length = count * tensor
    lead, slab, span = w_qkv.shape
    gain_count = gains.shape[0]
    half = slab // 2
    part_tall = span // 2
    heads = span // HEAD
    shard_units = w_gu.shape[2]
    units = shard_units // outer
    places = [(j, s) for j in range(inner) for s in range(outer) if not (j and s == outer - 1)]
    parts = len(places)
    ring = 2 * lead + 3
    steps = list(range(1, outer))
    tall = min(256, length)
    tile = 512
    lines = 32
    bf16, f32 = jnp.bfloat16, jnp.float32
    mesh_id = pl.DeviceIdType.MESH

    def kernel(*refs):
        body(*refs[:11], dict(zip(places, refs[11 : 11 + parts])), *refs[11 + parts :])

    def body(
        qkv_any, out_any, rows_any, gu_any, down_any, gains_ref, cos_ref, sin_ref, id_col, id_row, rows_ref,
        pieces, qkv_out, flat_out, seq_out,
        gain_rows, hat_ref, scale_ref, q_low, k_low, v_low, lse_ref, context, attn_hat, o_scale, resid, resid_low, top_ref,
        qkv_ref, out_w_ref, seq_ref, all_gains, qkv_wide, out_wide, gu_wide, down_wide, cast,
        square, squares, core_send, core_land, hold, chip_send, chip_land,
        s_ring, r_ring, s_row, r_row, s_z, r_z, s_y, r_y, s_sq, r_sq, s_core, r_core, s_chip, r_chip, local,
    ):
        g = Grid()

        def tensor_peer(k, flip):
            core = 1 - g.core_at if flip else g.core_at
            return (g.dp_at, lax.rem(g.chip_at + k + chips, chips) * 2 + core)

        def dp_peer(s, j):
            across = g.outer_flip(g.outer_at, s) * inner
            return (across + lax.rem(g.inner_at + j + inner, inner), g.tensor_at)

        near = [tensor_peer(k, f) for k in range(chips) for f in (0, 1) if (k, f) != (0, 0)]
        far = [dp_peer(s, 0) for s in range(1, outer)]
        far += [dp_peer(0, j) for j in sorted({1 % inner, inner - 1} - {0})]
        t_at = g.tensor_at
        place = g.path_of(g.dp_at)
        after = (g.index_of(lax.rem(place + 1, n)), t_at)
        before = (g.index_of(lax.rem(place + n - 1, n)), t_at)
        firsts = []
        for at, (src, dst) in enumerate(((qkv_any, qkv_wide), (out_any, out_wide))):
            firsts.append(pltpu.make_async_copy(src, dst, local.at[3 + at]))
            firsts[-1].start()
        greet(near + far + [after, before])

        def remote(src, dst, send, recv, peer):
            copy = pltpu.make_async_remote_copy(
                src_ref=src, dst_ref=dst, send_sem=send, recv_sem=recv,
                device_id=peer, device_id_type=mesh_id,
            )
            copy.start()
            return copy

        def dot(a, b, contract):
            return lax.dot_general(a, b, (contract, ((), ())), preferred_element_type=f32)

        def looped(total, make):
            lax.fori_loop(0, total, lambda i, c: (make(i), c)[1], 0, unroll=total <= 4)

        def rows_of(i, size):
            return pl.ds(pl.multiple_of(i * size, size), size)

        def fetch(src, dst, at):
            copy = pltpu.make_async_copy(src, dst, local.at[at])
            copy.start()
            return copy

        def views(item, index):
            if item == ring - 1:
                return 1, all_gains.at[index]
            if item >= 2 * lead:
                side = item - 2 * lead
                part = pl.ds(side * part_tall, part_tall)
                return 1 - 2 * side, out_w_ref.at[part, rows_of(index, slab)]
            side, c = item // lead, item % lead
            at = pl.ds(pl.multiple_of(index * slab + side * half, half), half)
            return 1 - 2 * side, qkv_ref.at[c, at]

        hops = {}

        def hop(step, item):
            way = views(item, 0)[0]
            index = g.index_of(lax.rem(place - way * step + n, n))
            _, view = views(item, index)
            hops[step, item] = remote(
                view,
                view,
                s_ring.at[step, item],
                r_ring.at[step, item],
                after if way == 1 else before,
            )

        def row_copy(slot, index, peer, src=None):
            at = seq_ref.at[rows_of(index, count)]
            return remote(at if src is None else src, at, s_row.at[slot], r_row.at[slot], peer)

        order = [c + side * lead for c in range(lead) for side in (0, 1)]
        order += list(range(2 * lead, ring))
        firsts[0].wait()
        for c in range(lead):

            def cast_own(i, c=c):
                at = rows_of(i, lines)
                there = pl.ds(pl.multiple_of(g.dp_at * slab + i * lines, lines), lines)
                qkv_ref[c, there] = qkv_wide[c, at].astype(bf16)

            looped(slab // lines, cast_own)
            for side in (0, 1):
                hop(0, c + side * lead)
        firsts[1].wait()

        def cast_flat(i):
            at = rows_of(i, lines)
            out_w_ref[at, rows_of(g.dp_at, slab)] = out_wide[at].astype(bf16)

        looped(span // lines, cast_flat)
        empty = jnp.zeros((16 - gain_count, slab), f32)
        all_gains[g.dp_at] = jnp.concatenate([gains_ref[...], empty], axis=0).astype(bf16)
        for item in range(2 * lead, ring):
            hop(0, item)
        row_copies = [
            row_copy(k - 1, t_at, tensor_peer(k, 0), rows_any) for k in range(1, chips)
        ]
        row_copies.append(row_copy(chips - 1, t_at, tensor_peer(0, 1), rows_any))
        wide = [fetch(gu_any, gu_wide, 1), fetch(down_any, down_wide, 2)]
        kept = fetch(rows_any, seq_ref.at[rows_of(t_at, count)], 5)

        def cast_wide(c):
            if c == 0:
                wide[0].wait()

            def cast_rows(i):
                at = rows_of(i, lines)
                cast[c, at] = gu_wide[c, at].astype(bf16)

            looped(slab // lines, cast_rows)

        def cast_turned():
            wide[1].wait()

            def cast_rows(i):
                at = rows_of(i, 256)
                cast[2, :, at] = down_wide[at].T.astype(bf16)

            looped(shard_units // 256, cast_rows)

        shadows = [lambda: cast_wide(0), lambda: cast_wide(1), cast_turned]
        for step in range(1, n - 1):
            for item in order:
                hops[step - 1, item].wait_recv()
                hop(step, item)
            if step <= chips - 1:
                row_copies[step - 1].wait_recv()
                source = lax.rem(g.chip_at - step + chips, chips) * 2 + g.core_at
                row_copies.append(row_copy(chips - 1 + step, source, tensor_peer(0, 1)))
            if shadows:
                shadows.pop(0)()

        def cut(s):
            return cast.at[:, :, rows_of(g.outer_flip(g.outer_at, s), units)]

        z_copies = {}

        for s in steps:
            z_copies[s] = remote(cut(s), pieces[0, s], s_z.at[s], r_z.at[s], dp_peer(s, 0))
        own = fetch(cut(0), pieces[0, 0], 0)
        y_copies = {}

        def pass_on(j, s):
            if (j, s) in pieces:
                src = cut(0) if (j, s) == (1, 0) else pieces[j - 1, s]
                y_copies[j, s] = remote(src, pieces[j, s], s_y.at[j, s], r_y.at[j, s], dp_peer(0, 1))

        pass_on(1, 0)
        duties = []
        for s in steps:

            def duty(s=s):
                z_copies[s].wait_recv()
                pass_on(1, s)

            duties.append(duty)
        for j in range(2, inner):
            for s in range(outer - 1):

                def duty(j=j, s=s):
                    y_copies[j - 1, s].wait_recv()
                    pass_on(j, s)

                duties.append(duty)

        def next_duties(times):
            for _ in range(times):
                if duties:
                    duties.pop(0)()

        for item in order:
            hops[n - 2, item].wait_recv()
        for copy in row_copies[chips - 1 :]:
            copy.wait_recv()
        kept.wait()
        outs = [fetch(qkv_ref, qkv_out, 3), fetch(out_w_ref, flat_out, 4), fetch(seq_ref, seq_out, 5)]

        def spread(i):
            gain_rows[:, rows_of(i, slab)] = all_gains[i].astype(f32)[:8]

        looped(n, spread)

        def project(i):
            at = rows_of(i, tall)
            x = seq_ref[at]
            lane = lax.broadcasted_iota(jnp.int32, (tall, 128), 1)
            sums = jnp.zeros((tall, 128), f32)
            for c in range(2):
                value = dot(x, qkv_ref[c], ((1,), (0,)))
                hat_ref[c, at] = value
                sums = jnp.where(lane == c, jnp.sum(value * value, axis=1, keepdims=True), sums)
            v_low[at] = dot(x, qkv_ref[2], ((1,), (0,))).astype(bf16)
            square[:, at] = sums.T[:8]

        looped(length // tall, project)
        sq_copies = []
        for k in range(chips):
            for f in (0, 1):
                if (k, f) != (0, 0):
                    at = k * 2 + f - 1
                    sq_copies.append(
                        remote(square, squares.at[at], s_sq.at[at], r_sq.at[at], tensor_peer(k, f))
                    )
        for copy in sq_copies:
            copy.wait_recv()
        sign = jnp.where(lax.broadcasted_iota(jnp.int32, (tall, HEAD), 1) < HEAD // 2, -1.0, 1.0)

        def rotate(i):
            at = rows_of(i, tall)
            sums = square[:, at]
            for copy_at in range(tensor - 1):
                sums = sums + squares[copy_at, :, at]
            column = jnp.concatenate([sums, jnp.zeros((120, tall), f32)], axis=0).T
            scales = lax.rsqrt(column / width + norm_eps)
            scale_ref[at] = scales
            cosine, sine = cos_ref[at], sin_ref[at] * sign
            for c, low in ((0, q_low), (1, k_low)):
                hat = hat_ref[c, at] * scales[:, c : c + 1]
                hat_ref[c, at] = hat
                normed = hat * gain_rows[c : c + 1, rows_of(t_at, span)]
                for h in range(heads):
                    cols = slice(h * HEAD, (h + 1) * HEAD)
                    value = normed[:, cols]
                    turned = pltpu.roll(value, HEAD // 2, 1)
                    low[at, cols] = (value * cosine + turned * sine).astype(bf16)

        looped(length // tall, rotate)
        scale = HEAD ** (-0.5)
        top_ref[...] = jnp.full((8, 128), masked_value, f32)
        for h in range(heads):
            cols = slice(h * HEAD, (h + 1) * HEAD)

            def attend(i, best, cols=cols, h=h):
                at = rows_of(i, tall)
                raw = dot(q_low[at, cols], k_low[:, cols], ((1,), (1,))) * scale
                masked = jnp.where(id_row[...] <= id_col[at], raw, masked_value)
                top = jnp.max(masked, axis=1, keepdims=True)
                weight = jnp.exp(masked - top)
                total = jnp.sum(weight, axis=1, keepdims=True)
                probs = (weight * (1.0 / total)).astype(bf16)
                context[at, cols] = dot(probs, v_low[:, cols], ((1,), (0,))).astype(bf16)
                lse_ref[at, h : h + 1] = top + jnp.log(total)
                return jnp.maximum(best, jnp.max(top, axis=0, keepdims=True))

            best = lax.fori_loop(
                0, length // tall, attend, jnp.full((1, 1), masked_value, f32), unroll=length // tall <= 4
            )
            top_ref[h : h + 1] = jnp.broadcast_to(best, (1, 128))
            if h + 1 == max(heads // 2, 1):
                next_duties(1)
        next_duties(1)

        def out_rows(k, flip, store):
            chip = lax.rem(g.chip_at + k, chips)
            core = 1 - g.core_at if flip else g.core_at
            at = rows_of(chip * 2 + core, count)

            def columns(i):
                cols = rows_of(i, tile)
                store(cols, dot(context[at], out_w_ref[:, cols], ((1,), (0,))))

            looped(width // tile, columns)

        chip_order = list(range(1, chips)) + [0]
        core_copies, chip_copies = {}, {}
        for k in chip_order:

            def store(cols, value, k=k):
                core_send[k, :, cols] = value.astype(bf16)

            out_rows(k, True, store)
            core_copies[k] = remote(
                core_send.at[k], core_land.at[k], s_core.at[k], r_core.at[k], tensor_peer(0, 1)
            )
        for k in chip_order:

            def store(cols, value, k=k):
                hold[k, :, cols] = value

            out_rows(k, False, store)
            if k:
                core_copies[k].wait_recv()

                def add(i, k=k):
                    at = rows_of(i, lines)
                    chip_send[k - 1, at] = (hold[k, at] + core_land[k, at].astype(f32)).astype(bf16)

                looped(count // lines, add)
                chip_copies[k] = remote(
                    chip_send.at[k - 1], chip_land.at[k - 1], s_chip.at[k], r_chip.at[k], tensor_peer(k, 0)
                )
        core_copies[0].wait_recv()
        for k in range(1, chips):
            chip_copies[k].wait_recv()

        def close(i):
            at = rows_of(i, lines)
            raw = hold[0, at] + core_land[0, at].astype(f32)
            for k in range(1, chips):
                raw = raw + chip_land[k - 1, at].astype(f32)
            scale_o = lax.rsqrt(jnp.mean(raw * raw, axis=1, keepdims=True) + norm_eps)
            hat = raw * scale_o
            attn_hat[at] = hat
            o_scale[at] = scale_o
            value = rows_ref[at].astype(f32) + hat * gain_rows[2:3]
            resid[at] = value
            resid_low[at] = value.astype(bf16)

        looped(count // lines, close)
        next_duties(len(duties))
        own.wait()
        for key, copy in y_copies.items():
            if key[0] == inner - 1:
                copy.wait_recv()
        for copy in outs:
            copy.wait()
        sent = list(hops.values()) + row_copies + list(z_copies.values()) + list(y_copies.values()) + sq_copies
        for copy in sent + list(core_copies.values()) + list(chip_copies.values()):
            copy.wait_send()

    shape = jax.ShapeDtypeStruct
    anywhere = pl.BlockSpec(memory_space=pl.ANY)
    vmem = pl.BlockSpec(memory_space=pltpu.VMEM)
    sems = pltpu.SemaphoreType.DMA
    results = pl.pallas_call(
        kernel,
        out_shape=(shape((3, slab, units), bf16),) * parts
        + (
            shape((lead, width, span), bf16),
            shape((span, width), bf16),
            shape((length, width), bf16),
            shape((8, width), f32),
            shape((2, length, span), f32),
            shape((length, 128), f32),
            shape((length, span), bf16),
            shape((length, span), bf16),
            shape((length, span), bf16),
            shape((length, heads), f32),
            shape((length, span), bf16),
            shape((count, width), f32),
            shape((count, 1), f32),
            shape((count, width), f32),
            shape((count, width), bf16),
            shape((8, 128), f32),
        ),
        in_specs=[anywhere] * 5 + [vmem] * 6,
        out_specs=(anywhere,) * (parts + 3) + (vmem,) * 13,
        scratch_shapes=[
            pltpu.VMEM((lead, width, span), bf16),
            pltpu.VMEM((span, width), bf16),
            pltpu.VMEM((length, width), bf16),
            pltpu.VMEM((n, 16, slab), bf16),
            pltpu.VMEM(w_qkv.shape, f32),
            pltpu.VMEM(w_out.shape, f32),
            pltpu.VMEM(w_gu.shape, f32),
            pltpu.VMEM(w_down.shape, f32),
            pltpu.VMEM((3, slab, shard_units), bf16),
            pltpu.VMEM((8, length), f32),
            pltpu.VMEM((tensor - 1, 8, length), f32),
            pltpu.VMEM((chips, count, width), bf16),
            pltpu.VMEM((chips, count, width), bf16),
            pltpu.VMEM((chips, count, width), f32),
            pltpu.VMEM((max(chips - 1, 1), count, width), bf16),
            pltpu.VMEM((max(chips - 1, 1), count, width), bf16),
            sems((n - 1, ring)),
            sems((n - 1, ring)),
            sems((2 * chips - 1,)),
            sems((2 * chips - 1,)),
            sems((outer,)),
            sems((outer,)),
            sems((inner, outer)),
            sems((inner, outer)),
            sems((tensor - 1,)),
            sems((tensor - 1,)),
            sems((chips,)),
            sems((chips,)),
            sems((chips,)),
            sems((chips,)),
            sems((7,)),
        ],
        compiler_params=pltpu.CompilerParams(
            collective_id=0, has_side_effects=True, vmem_limit_bytes=58 * 2**20
        ),
    )(
        w_qkv, w_out, rows, w_gu, w_down, gains, tables[0], tables[1],
        blocks[:, None], blocks[None, :], rows,
    )
    return dict(zip(places, results[:parts])), results[parts:]


def unit_kernel_call(rows_low, resid, cotangent, gain, pieces):
    grid = Grid()
    outer, chips, inner = grid.outer, grid.chips, grid.inner
    total_rows, width = rows_low.shape
    slab, units = pieces[0, 0].shape[1:]
    places = list(pieces)
    parts = len(places)
    last = (0, outer - 1)
    halves = 2
    count = total_rows // halves
    both = 2 * count
    per = min(2, chips)
    groups = chips // per
    blocks = outer * groups
    tall = per * both
    held = per if groups > 1 else max(per - 1, 1)
    links = outer * (chips - 1)
    steps = list(range(outer))
    far_first = [0] + steps[2:] + steps[1:2]

    def units_of(of_steps):
        return [(s, i) for s in of_steps for i in range(groups)]

    orders = {
        (0, 0): units_of(far_first),
        (0, 1): units_of(far_first),
        (1, 0): units_of(steps),
        (1, 1): units_of(far_first),
    }
    grad_order = units_of(far_first)
    tile = 512
    wide_tiles = width // tile
    unit_tile = min(256, units)
    lines = 32
    bf16, f32 = jnp.bfloat16, jnp.float32
    mesh_id = pl.DeviceIdType.MESH

    def plan():
        chip_us, core_us, hop_us = 5.6, 0.6, 2.0
        free = {"x": 0.0, "core": 0.0, "z near": 0.0, "z far": 0.0}
        arrive, done, tasks = {("w",): 20.0}, {}, {}

        def send(link, when, us):
            free[link] = max(free[link], when) + us
            return free[link] + hop_us

        def add(name, needs, us, after=None):
            tasks[name] = (needs, us, after)

        def send_outer(s, now):
            return send("z near", now, 8.0) if s == 1 else send("z far", now, 10.5)

        def go(p, h):
            def then(now):
                if (p, h) != (0, 1):
                    for s in steps[1:]:
                        arrive["z", p, h, s] = send_outer(s, now)
                for k in range(1, chips):
                    arrive["x", p, h, 0, k] = send("x", now, chip_us)
                arrive["c", p, h, 0, 0] = send("core", now, core_us)

            return then

        def zf(p, h, s):
            def then(now):
                for k in range(1, chips):
                    arrive["x", p, h, s, k] = send("x", now, chip_us)
                arrive["c", p, h, s, 0] = send("core", now, core_us)
                if (p, h) == (0, 0):
                    arrive["z", 0, 1, s] = send_outer(s, now)

            return then

        def xf(p, h, s, k):
            def then(now):
                arrive["c", p, h, s, k] = send("core", now, core_us)

            return then

        def compute(p, h, s, i):
            def then(now):
                arrive["cr", p, h, s, i] = send("core", now, per * core_us)

            return then

        def cr(p, h, s, i):
            def then(now):
                for k in range(i * per, i * per + per):
                    if k:
                        arrive["xr", p, h, s, k] = send("x", now, chip_us)

            return then

        def xr(p, h, s):
            def then(now):
                if s:
                    arrive["zr", p, h, s] = send_outer(s, now)

            return then

        for p in (0, 1):
            for h in range(halves):
                if p == 0:
                    needs = [("do", ("go", 0, h - 1))] if h else []
                else:
                    needs = [("do", ("between", h))]
                add(("go", p, h), needs, 0.2, go(p, h))
                for s in steps[1:]:
                    add(("zf", p, h, s), [("at", ("z", p, h, s))], 0.2, zf(p, h, s))
                for s in steps:
                    for k in range(1, chips):
                        add(("xf", p, h, s, k), [("at", ("x", p, h, s, k))], 0.2, xf(p, h, s, k))
                order = orders[p, h]
                for n, (s, i) in enumerate(order):
                    needs = [("at", ("c", p, h, s, i * per + j)) for j in range(per)]
                    if n:
                        needs.append(("do", ("front", p, h) + order[n - 1]))
                    add(("load", p, h, s, i), needs, 0.2)
                    needs = [("do", ("load", p, h, s, i)), ("do", ("weights",))]
                    add(("front", p, h, s, i), needs, (2.4, 1.6)[p])
                    needs = [("do", ("front", p, h, s, i))]
                    if n:
                        needs.append(("do", ("cr", p, h) + order[n - 1]))
                    add(("compute", p, h, s, i), needs, (1.6, 2.4)[p], compute(p, h, s, i))
                    needs = [("at", ("cr", p, h, s, i)), ("do", ("compute", p, h, s, i))]
                    add(("cr", p, h, s, i), needs, 0.5, cr(p, h, s, i))
                for s in steps:
                    needs = [("do", ("cr", p, h, s, 0))]
                    needs += [("at", ("xr", p, h, s, k)) for k in range(1, chips)]
                    add(("xr", p, h, s), needs, 0.4, xr(p, h, s))
                for s in steps[1:]:
                    needs = [("at", ("zr", p, h, s)), ("do", ("xr", p, h, 0))]
                    add(("zr", p, h, s), needs, 0.4)
        add(("weights",), [("at", ("w",))], 0.2)
        for h in range(halves):
            needs = [("do", ("zr", 0, h, s)) for s in steps[1:]] + [("do", ("xr", 0, h, 0))]
            add(("between", h), needs, 1.0)
        for n, (s, i) in enumerate(grad_order):
            needs = [("do", ("compute", 1, h, s, i)) for h in range(halves)]
            if n:
                needs.append(("do", ("grads",) + grad_order[n - 1] + (2,)))
            add(("fetch", s, i), needs, 0.2)
            for c in range(3):
                needs = [("do", ("grads", s, i, c - 1) if c else ("fetch", s, i))]
                add(("grads", s, i, c), needs, 2.8)
        written = [(j, s) for j in range(inner) for s in range(outer)]
        for n, at in enumerate(written):
            needs = [("do", ("grads",) + grad_order[-1] + (2,))]
            if n:
                needs = [("do", ("write",) + written[n - 1])]
            add(("write",) + at, needs, 0.6)
        rank = {"compute": 1, "front": 2, "fetch": 2, "grads": 3, "write": 4}
        result = []
        now = 0.0
        while tasks:
            best = None
            for name, (needs, us, then) in tasks.items():
                ready = 0.0
                for kind, key in needs:
                    table = arrive if kind == "at" else done
                    if key not in table:
                        ready = None
                        break
                    ready = max(ready, table[key] + (1.0 if key[0] in ("load", "fetch") else 0.0))
                if ready is None:
                    continue
                key = (max(ready, now), rank.get(name[0], 0))
                if best is None or key < best[0]:
                    best = (key, name)
            (ready, _), name = best
            needs, us, then = tasks.pop(name)
            now = ready + us
            done[name] = now
            if then is not None:
                then(now)
            result.append(name)
        return result

    def kernel(*refs):
        piece_refs = dict(zip(places, refs[:parts]))
        fixed = refs[parts : parts + 9]
        k = parts + 9
        late, grad_refs = refs[k : k + inner - 1], refs[k + inner - 1 : k + inner - 1 + 3 * inner]
        for j in range(1, inner):
            piece_refs[j, outer - 1] = late[j - 1]
        body(piece_refs, *fixed, grad_refs, *refs[k + inner - 1 + 3 * inner :])

    def body(
        piece_refs, rows_ref, resid_ref, cot_ref, gain_ref,
        out_ref, dres_ref, gain_out, all_x, all_dm, grad_refs,
        wg, wu, wd, buf, wide_buf, act, coef_gate, coef_up, d_gate, d_up, turned, acc_gate, acc_up, acc_down, stage, stage_down,
        core_send, core_land, hold, keep, chip_send, chip_land, outer_send, outer_land, raw, d_mlp,
        s_outer, r_outer, s_chip, r_chip, s_core, r_core,
        s_core_sum, r_core_sum, s_chip_sum, r_chip_sum, s_outer_sum, r_outer_sum,
        local, local_own, local_wide, local_w, local_g, s_late, r_late,
    ):
        g = Grid()
        core_peer = (g.dp_at, g.chip_at * 2 + 1 - g.core_at)

        def chip_peer(k):
            return (g.dp_at, lax.rem(g.chip_at + k + chips, chips) * 2 + g.core_at)

        def outer_peer(s):
            return (g.outer_flip(g.outer_at, s) * inner + g.inner_at, g.tensor_at)

        def inner_peer(j):
            return (g.outer_at * inner + lax.rem(g.inner_at + j, inner), g.tensor_at)

        greet(
            [core_peer]
            + [chip_peer(k) for k in range(1, chips)]
            + [outer_peer(s) for s in range(1, outer)]
            + [inner_peer(j) for j in range(1, inner)]
        )

        def remote(src, dst, send, recv, peer):
            copy = pltpu.make_async_remote_copy(
                src_ref=src, dst_ref=dst, send_sem=send, recv_sem=recv,
                device_id=peer, device_id_type=mesh_id,
            )
            copy.start()
            return copy

        def fetch(src, dst, sem):
            copy = pltpu.make_async_copy(src, dst, sem)
            copy.start()
            return copy

        def dot(a, b, contract):
            return lax.dot_general(a, b, (contract, ((), ())), preferred_element_type=f32)

        def looped(total, make):
            lax.fori_loop(0, total, lambda i, c: (make(i), c)[1], 0, unroll=total <= 4)

        def by_lines(make):
            looped(count // lines, lambda i: make(pl.ds(pl.multiple_of(i * lines, lines), lines)))

        def by_tiles(make):
            looped(wide_tiles, lambda i: make(pl.ds(pl.multiple_of(i * tile, tile), tile)))

        weights = (wg, wu, wd)
        fetches = []

        late_copies = []

        def send_late():
            for j in range(1, inner):
                late_copies.append(
                    remote(piece_refs[last], piece_refs[j, last[1]], s_late.at[j], r_late.at[j], inner_peer(j))
                )

        def fetch_weights(which):
            for j, s in which:
                index = g.outer_flip(g.outer_at, s) * inner
                index = index + lax.rem(g.inner_at - j + inner, inner)
                span = pl.ds(pl.multiple_of(index * slab, slab), slab)
                for c in range(3):
                    fetches.append(
                        fetch(piece_refs[j, s].at[c], weights[c].at[span], local_w.at[j * outer + s, c])
                    )

        mine, theirs = pl.ds(0, count), pl.ds(count, count)
        every = (all_x, all_dm)
        copies, sums, loads, own = {}, {}, {}, {}
        unsent = {(p, h): [] for p in (0, 1) for h in range(halves)}

        def track(p, h, copy):
            unsent[p, h].append(copy)
            return copy

        def core_copy(p, h, s, k, src):
            dst = every[p].at[h, s, k, theirs]
            copies["c", p, h, s, k] = track(
                p, h, remote(src, dst, s_core.at[p, h, s, k], r_core.at[p, h, s, k], core_peer)
            )

        def chip_copy(p, h, s, k, src):
            dst = every[p].at[h, s, k, mine]
            copies["x", p, h, s, k] = track(
                p, h, remote(src, dst, s_chip.at[p, h, s, k], r_chip.at[p, h, s, k], chip_peer(k))
            )

        def outer_copy(p, h, s):
            source = (rows_ref, d_mlp)[p].at[pl.ds(h * count, count)]
            dst = every[p].at[h, s, 0, mine]
            copies["z", p, h, s] = track(
                p, h, remote(source, dst, s_outer.at[p, h, s], r_outer.at[p, h, s], outer_peer(s))
            )

        def go(p, h):
            source = (rows_ref, d_mlp)[p].at[pl.ds(h * count, count)]
            if (p, h) != (0, 1):
                for s in steps[1:]:
                    outer_copy(p, h, s)
            for k in range(1, chips):
                chip_copy(p, h, 0, k, source)
            core_copy(p, h, 0, 0, source)
            own[p, h] = fetch(source, every[p].at[h, 0, 0, mine], local_own.at[p, h])
            if p == 0 and h == 0:
                fetch_weights(places)

        def part_out(h, s, i, cols, part_sum):
            for j in range(per):
                own_rows = part_sum[j * both : j * both + count]
                if i * per + j == 0:
                    keep[h, s, :, cols] = own_rows
                else:
                    hold[h, min(j, held - 1), :, cols] = own_rows
                core_send[h, j, :, cols] = part_sum[j * both + count : (j + 1) * both].astype(bf16)

        def forward(h, unit):
            for j in range(units // unit_tile):
                cols = pl.ds(j * unit_tile, unit_tile)
                rows = buf[h].reshape(tall, width)
                gate = dot(rows, wg[:, cols], ((1,), (0,)))
                up = dot(rows, wu[:, cols], ((1,), (0,)))
                sigma = jax.nn.sigmoid(gate)
                silu = gate * sigma
                act[unit, h, :, cols] = (silu * up).astype(bf16)
                coef_up[unit, h, :, cols] = silu.astype(bf16)
                coef_gate[unit, h, :, cols] = (
                    up * sigma * (1.0 + gate * (1.0 - sigma))
                ).astype(bf16)

        def forward_out(h, unit, s, i):
            by_tiles(
                lambda cols: part_out(h, s, i, cols, dot(act[unit, h], wd[cols, :], ((1,), (1,))))
            )

        def backward(h, unit):
            for j in range(units // unit_tile):
                cols = pl.ds(j * unit_tile, unit_tile)
                d_act = dot(buf[h].reshape(tall, width), wd[:, cols], ((1,), (0,)))
                d_gate[unit, h, :, cols] = (d_act * coef_gate[unit, h, :, cols].astype(f32)).astype(bf16)
                d_up[unit, h, :, cols] = (d_act * coef_up[unit, h, :, cols].astype(f32)).astype(bf16)

        def backward_out(h, unit, s, i):
            def into(cols):
                part_sum = dot(d_gate[unit, h], wg[cols, :], ((1,), (1,)))
                part_sum = part_sum + dot(d_up[unit, h], wu[cols, :], ((1,), (1,)))
                part_out(h, s, i, cols, part_sum)

            by_tiles(into)

        def weight_grads(unit, c):
            first = unit == grad_order[0][0] * groups + grad_order[0][1]
            left, right, acc = ((d_gate, 0, acc_gate), (d_up, 0, acc_up), (act, 1, acc_down))[c]
            turned[...] = left[unit].reshape(halves * tall, units).T

            def grads(cols):
                rows = wide_buf[right, :, :, :, cols].reshape(halves * tall, tile)
                value = dot(turned[...], rows, ((1,), (0,)))
                acc[:, cols] = value if first else acc[:, cols] + value

            by_tiles(grads)

        def between(h):
            def lines_of(i, total):
                at_rows = pl.ds(pl.multiple_of(h * count + i * lines, lines), lines)
                value = raw[at_rows]
                scale = lax.rsqrt(jnp.mean(value * value, axis=1, keepdims=True) + norm_eps)
                hat = value * scale
                gain_row = gain_ref[3:4]
                out_ref[at_rows] = (resid_ref[at_rows] + hat * gain_row).astype(bf16)
                top = cot_ref[at_rows].astype(f32)
                upstream = top * gain_row
                mean = jnp.mean(upstream * hat, axis=1, keepdims=True)
                d_mlp[at_rows] = (scale * (upstream - hat * mean)).astype(bf16)
                return total + jnp.sum(top * hat, axis=0, keepdims=True)

            zero = jnp.zeros((1, width), f32)
            total = lax.fori_loop(0, count // lines, lines_of, zero)
            gain_out[...] = total if h == 0 else gain_out[...] + total

        batches = []

        def write_grads(j, s):
            index = g.outer_flip(g.outer_at, s) * inner
            index = index + lax.rem(g.inner_at + j, inner)
            span = pl.ds(pl.multiple_of(index * slab, slab), slab)
            for copy in batches:
                copy.wait()
            batches.clear()
            for c, src in enumerate((stage.at[0], stage.at[1], stage_down)):
                if c == 0:
                    stage[0] = acc_gate[:, span].astype(bf16).T
                elif c == 1:
                    stage[1] = acc_up[:, span].astype(bf16).T
                else:
                    stage_down[...] = acc_down[:, span].astype(bf16)
                batches.append(fetch(src, grad_refs[j * 3 + c].at[s], local_g.at[c]))

        def core_sum(p, h, s, i):
            unit = s * groups + i
            sums["c", p, h, unit].wait_recv()
            for j in range(per):
                chip = i * per + j
                if chip == 0:

                    def add(at_rows):
                        keep[h, s, at_rows] = keep[h, s, at_rows] + core_land[h, unit, j, at_rows].astype(f32)

                    by_lines(add)
                    continue
                there = s * (chips - 1) + chip - 1

                def add(at_rows):
                    total = hold[h, min(j, held - 1), at_rows] + core_land[h, unit, j, at_rows].astype(f32)
                    chip_send[h, there, at_rows] = total.astype(bf16)

                by_lines(add)
                sums["x", p, h, s, chip] = track(
                    p, h,
                    remote(
                        chip_send.at[h, there], chip_land.at[h, there],
                        s_chip_sum.at[p, h, there], r_chip_sum.at[p, h, there], chip_peer(-chip),
                    ),
                )

        def chip_sum(p, h, s):
            for k in range(1, chips):
                sums["x", p, h, s, k].wait_recv()

            def add(at_rows):
                total = keep[h, s, at_rows]
                for k in range(1, chips):
                    total = total + chip_land[h, s * (chips - 1) + k - 1, at_rows].astype(f32)
                if s == 0:
                    raw[pl.ds(pl.multiple_of(h * count + at_rows.start, lines), lines)] = total
                else:
                    outer_send[h, s - 1, at_rows] = total.astype(bf16)

            by_lines(add)
            if s:
                sums["z", p, h, s] = track(
                    p, h,
                    remote(
                        outer_send.at[h, s - 1], outer_land.at[h, s - 1],
                        s_outer_sum.at[p, h, s], r_outer_sum.at[p, h, s], outer_peer(s),
                    ),
                )

        def outer_sum(p, h, s):
            sums["z", p, h, s].wait_recv()

            def add(at_rows):
                there = pl.ds(pl.multiple_of(h * count + at_rows.start, lines), lines)
                raw[there] = raw[there] + outer_land[h, s - 1, at_rows].astype(f32)

            by_lines(add)

        def all_sent(p, h):
            for copy in unsent[p, h]:
                copy.wait_send()

        last_core = {}
        send_late()
        for task in plan():
            name, args = task[0], task[1:]
            if name == "go":
                go(*args)
            elif name == "zf":
                p, h, s = args
                copies["z", p, h, s].wait_recv()
                source = every[p].at[h, s, 0, mine]
                for k in range(1, chips):
                    chip_copy(p, h, s, k, source)
                core_copy(p, h, s, 0, source)
                if (p, h) == (0, 0):
                    outer_copy(0, 1, s)
            elif name == "xf":
                p, h, s, k = args
                copies["x", p, h, s, k].wait_recv()
                core_copy(p, h, s, k, every[p].at[h, s, k, mine])
            elif name == "load":
                p, h, s, i = args
                for j in range(per):
                    copies["c", p, h, s, i * per + j].wait_recv()
                if (s, i) == (0, 0):
                    own[p, h].wait()
                src = every[p].at[h, s, pl.ds(i * per, per)]
                loads[args] = fetch(src, buf.at[h], local.at[p, h, s * groups + i])
            elif name == "weights":
                for copy in late_copies:
                    copy.wait_recv()
                fetch_weights([(j, last[1]) for j in range(1, inner)])
            elif name == "front":
                p, h, s, i = args
                if p == 0 and not loads.get("weights"):
                    loads["weights"] = True
                    for copy in fetches:
                        copy.wait()
                loads[args].wait()
                (forward, backward)[p](h, s * groups + i)
            elif name == "compute":
                p, h, s, i = args
                unit = s * groups + i
                if h in last_core:
                    last_core[h].wait_send()
                (forward_out, backward_out)[p](h, unit, s, i)
                last_core[h] = remote(
                    core_send.at[h], core_land.at[h, unit],
                    s_core_sum.at[p, h, unit], r_core_sum.at[p, h, unit], core_peer,
                )
                sums["c", p, h, unit] = last_core[h]
            elif name == "cr":
                core_sum(*args)
            elif name == "xr":
                chip_sum(*args)
            elif name == "zr":
                outer_sum(*args)
            elif name == "between":
                all_sent(0, args[0])
                between(args[0])
            elif name == "fetch":
                s, i = args
                loads[task] = []
                for at, src in enumerate((all_x, all_dm)):
                    for h in range(halves):
                        loads[task].append(
                            fetch(
                                src.at[h, s, pl.ds(i * per, per)],
                                wide_buf.at[at, h],
                                local_wide.at[s * groups + i, at * halves + h],
                            )
                        )
            elif name == "grads":
                s, i, c = args
                if c == 0:
                    for copy in loads["fetch", s, i]:
                        copy.wait()
                weight_grads(s * groups + i, c)
            elif name == "write":
                write_grads(*args)

        looped(
            total_rows // lines,
            lambda i: close_rows(pl.ds(pl.multiple_of(i * lines, lines), lines), dres_ref, raw, cot_ref),
        )
        for h in range(halves):
            all_sent(1, h)
            last_core[h].wait_send()
        for copy in batches:
            copy.wait()
        for copy in late_copies:
            copy.wait_send()

    shape = jax.ShapeDtypeStruct
    anywhere = pl.BlockSpec(memory_space=pl.ANY)
    near = pl.BlockSpec(memory_space=pltpu.VMEM)
    sems = pltpu.SemaphoreType.DMA
    flops = 2 * 9 * halves * tall * blocks * width * units
    results = pl.pallas_call(
        kernel,
        out_shape=(
            shape((total_rows, width), bf16),
            shape((total_rows, width), f32),
            shape((1, width), f32),
            shape((halves, outer, chips, both, width), bf16),
            shape((halves, outer, chips, both, width), bf16),
        )
        + (shape((3, slab, units), bf16),) * (inner - 1)
        + (
            shape((outer, slab, units), bf16),
            shape((outer, slab, units), bf16),
            shape((outer, units, slab), bf16),
        )
        * inner,
        in_specs=[anywhere] * (parts + 1) + [near] * 3,
        out_specs=(near, near, near) + (anywhere,) * (2 + inner - 1 + 3 * inner),
        scratch_shapes=[
            pltpu.VMEM((width, units), bf16),
            pltpu.VMEM((width, units), bf16),
            pltpu.VMEM((width, units), bf16),
            pltpu.VMEM((halves, per, both, width), bf16),
            pltpu.VMEM((2, halves, per, both, width), bf16),
            pltpu.VMEM((blocks, halves, tall, units), bf16),
            pltpu.VMEM((blocks, halves, tall, units), bf16),
            pltpu.VMEM((blocks, halves, tall, units), bf16),
            pltpu.VMEM((blocks, halves, tall, units), bf16),
            pltpu.VMEM((blocks, halves, tall, units), bf16),
            pltpu.VMEM((units, halves * tall), bf16),
            pltpu.VMEM((units, width), f32),
            pltpu.VMEM((units, width), f32),
            pltpu.VMEM((units, width), f32),
            pltpu.VMEM((2, slab, units), bf16),
            pltpu.VMEM((units, slab), bf16),
            pltpu.VMEM((halves, per, count, width), bf16),
            pltpu.VMEM((halves, blocks, per, count, width), bf16),
            pltpu.VMEM((halves, held, count, width), f32),
            pltpu.VMEM((halves, outer, count, width), f32),
            pltpu.VMEM((halves, links, count, width), bf16),
            pltpu.VMEM((halves, links, count, width), bf16),
            pltpu.VMEM((halves, outer - 1, count, width), bf16),
            pltpu.VMEM((halves, outer - 1, count, width), bf16),
            pltpu.VMEM((total_rows, width), f32),
            pltpu.VMEM((total_rows, width), bf16),
            sems((2, halves, outer)),
            sems((2, halves, outer)),
            sems((2, halves, outer, chips)),
            sems((2, halves, outer, chips)),
            sems((2, halves, outer, chips)),
            sems((2, halves, outer, chips)),
            sems((2, halves, blocks)),
            sems((2, halves, blocks)),
            sems((2, halves, links)),
            sems((2, halves, links)),
            sems((2, halves, outer)),
            sems((2, halves, outer)),
            sems((2, halves, blocks)),
            sems((2, halves)),
            sems((blocks, 2 * halves)),
            sems((inner * outer, 3)),
            sems((3,)),
            sems((inner,)),
            sems((inner,)),
        ],
        compiler_params=pltpu.CompilerParams(
            collective_id=2, has_side_effects=True, vmem_limit_bytes=62 * 2**20
        ),
        cost_estimate=pl.CostEstimate(flops=flops, bytes_accessed=64 * 2**20, transcendentals=0),
    )(*pieces.values(), rows_low, resid, cotangent, gain)
    grads = results[5 + inner - 1 :]
    return results[:3] + ([[grads[j * 3 + c] for j in range(inner)] for c in range(3)],)


def close_rows(at_rows, dres_ref, raw, cot_ref):
    dres_ref[at_rows] = raw[at_rows] + cot_ref[at_rows].astype(jnp.float32)


def local(
    tokens,
    cotangent,
    block_ids,
    w_qkv,
    m_qkv,
    v_qkv,
    w_out,
    m_out,
    v_out,
    w_gu,
    m_gu,
    v_gu,
    w_down,
    m_down,
    v_down,
    gains,
    gain_m,
    gain_v,
):
    grid = Grid()
    local_x = tokens[0]
    gain_count = gains.shape[0]
    tables = rope_tables(local_x.shape[0] * grid.tensor, HEAD)
    pieces, kept = open_call(
        w_qkv,
        w_out,
        gains,
        local_x,
        w_gu,
        w_down,
        tables,
        block_ids[0],
    )
    full_qkv, full_out, seq_x, gain_rows = kept[:4]
    hats, scales, q_low, k_low, v_low, log_total, context_low = kept[4:11]
    attn_hat, o_scale, resid, resid_low, tops = kept[11:]
    output, d_resid, gain_last, unit_grads = unit_kernel_call(
        resid_low, resid, cotangent[0], gain_rows, pieces
    )
    part_gu, part_down, part_qkv, part_out, part_gains, tops, grad_tokens = attend_back_call(
        d_resid,
        attn_hat,
        o_scale,
        gain_rows,
        full_out,
        context_low,
        q_low,
        k_low,
        v_low,
        log_total,
        hats,
        scales,
        tables,
        block_ids[0],
        seq_x,
        full_qkv,
        gain_last,
        tops,
        unit_grads,
    )
    part_gains = part_gains[:gain_count]
    head_top = tops[: w_qkv.shape[2] // HEAD, 0]
    factor = clip_tau / jnp.maximum(head_top, clip_tau)
    column = jnp.repeat(jnp.sqrt(factor), HEAD)
    column_scale = jnp.stack([column, column, jnp.ones_like(column)])[:, None, :]
    new_qkv, new_m_qkv, new_v_qkv = adam_step(
        w_qkv, part_qkv, m_qkv, v_qkv, rate_matrix, weight_decay
    )
    new_qkv = new_qkv * column_scale
    new_out, new_m_out, new_v_out = adam_step(
        w_out, part_out, m_out, v_out, rate_matrix, weight_decay
    )
    new_gu, new_m_gu, new_v_gu = adam_step(
        w_gu, part_gu.astype(jnp.float32), m_gu, v_gu, rate_matrix, weight_decay
    )
    new_down, new_m_down, new_v_down = adam_step(
        w_down, part_down.astype(jnp.float32), m_down, v_down, rate_matrix, weight_decay
    )
    new_gains, new_gain_m, new_gain_v = adam_step(gains, part_gains, gain_m, gain_v, rate_gain, 0.0)
    return (
        output[None],
        grad_tokens[None],
        new_qkv,
        new_m_qkv,
        new_v_qkv,
        new_qkv.astype(jnp.bfloat16),
        new_out,
        new_m_out,
        new_v_out,
        new_out.astype(jnp.bfloat16),
        new_gu,
        new_m_gu,
        new_v_gu,
        new_gu.astype(jnp.bfloat16),
        new_down,
        new_m_down,
        new_v_down,
        new_down.astype(jnp.bfloat16),
        new_gains,
        new_gain_m,
        new_gain_v,
        factor,
    )


def solution(mesh):
    return jax.shard_map(
        local,
        mesh=mesh,
        in_specs=(
            P("dp", "tensor", None),
            P("dp", "tensor", None),
            P("dp", None),
            P(None, "dp", "tensor"),
            P(None, "dp", "tensor"),
            P(None, "dp", "tensor"),
            P("tensor", "dp"),
            P("tensor", "dp"),
            P("tensor", "dp"),
            P(None, "dp", "tensor"),
            P(None, "dp", "tensor"),
            P(None, "dp", "tensor"),
            P("tensor", "dp"),
            P("tensor", "dp"),
            P("tensor", "dp"),
            P(None, "dp"),
            P(None, "dp"),
            P(None, "dp"),
        ),
        out_specs=(
            P("dp", "tensor", None),
            P("dp", "tensor", None),
            P(None, "dp", "tensor"),
            P(None, "dp", "tensor"),
            P(None, "dp", "tensor"),
            P(None, "dp", "tensor"),
            P("tensor", "dp"),
            P("tensor", "dp"),
            P("tensor", "dp"),
            P("tensor", "dp"),
            P(None, "dp", "tensor"),
            P(None, "dp", "tensor"),
            P(None, "dp", "tensor"),
            P(None, "dp", "tensor"),
            P("tensor", "dp"),
            P("tensor", "dp"),
            P("tensor", "dp"),
            P("tensor", "dp"),
            P(None, "dp"),
            P(None, "dp"),
            P(None, "dp"),
            P("tensor"),
        ),
        check_vma=False,
    )
```

profile of v0, /device:TPU:13, one launch (start us, length us, event | category | flops | bytes accessed | tf_op | source)
XLA Modules:
  0.0 594.9 jit_solution(489164810945849347)
XLA Ops:
  0.7 1.5 copy.42.refs_8_.refs_13_
  2.2 157.3 %shard_map.363 = (bf16[3,256,512]{2,1,0:T(8,128)(2,1)}, bf16[3,256,512]{2,1,0:T(8,128)(2,1)}, bf16[3,256,512]{2,1,0:T(8,128)(2,1)}, bf16[3,256,512]{2,1,0:T(8,12...) custom-call(f32[3,256,512]{2,1,0:T(8,128)} %refs_0_.1, ...), custom_call_target="tpu_custom_call" | custom-call | tf_op jit(solution)/shard_map/pallas_call | solution.py:978
  159.5 230.0 %shard_map.364 = (bf16[128,2048]{1,0:T(8,128)(2,1)}, f32[128,2048]{1,0:T(8,128)}, f32[1,2048]{1,0:T(1,128)}, bf16[2,4,2,128,2048]{4,3,2,1,0:T(8,128)(2,1)}, bf16...) custom-call(bf16[3,256,512]{2,1,0:T(8,128)(2,1)} %get-tuple-element., ...), custom_call_target="tpu_custom_call" | custom-call | flops 38654705664 | bytes 67108864 | tf_op jit(solution)/shard_map/pallas_call | solution.py:1596
  389.5 179.9 %shard_map.365 = (bf16[2,256,2048]{2,1,0:T(8,128)(2,1)}, bf16[2048,256]{1,0:T(8,128)(2,1)}, f32[3,256,512]{2,1,0:T(8,128)}, f32[512,256]{1,0:T(8,128)}, f32[8,25...) custom-call(f32[128,2048]{1,0:T(8,128)} %get-tuple-element.72.refs_0_, f32[128,2048]{1,0:T(8,128)} %get-tuple-element.73.refs_1_, ...), custom_call_target="tpu_custom_call" | custom-call | tf_op jit(solution)/shard_map/pallas_call | solution.py:543
  569.4 0.0 copy-start
  569.5 0.0 copy-start.2
  569.5 0.0 copy-start.3
  569.5 0.0 copy-start.8
  569.5 11.6 %fusion.12 = (bf16[2,256,2048]{2,1,0:T(8,128)(2,1)}, f32[2,256,2048]{2,1,0:T(8,128)}, f32[2,256,2048]{2,1,0:T(8,128)}, f32[2,256,2048]{2,1,0:T(8,128)}) fusion(f32[2,256,2048]{2,1,0:T(8,128)} %refs_3_.1, bf16[2,256,2048]{2,1,0:T(8,128)(2,1)} %get-tuple-element.97, f32[2,256,2048]{2,1,0:T(8,128)} %param.30, f32[2,256,2048]{2,1,0:T(8,128)} %param.31), kind=kLoop, calls=%fused_computation.26 | loop fusion | flops 17825792 | bytes 29360128 | tf_op jit(solution)/shard_map/convert_element_type | solution.py:1768
  581.1 0.0 copy-done
  581.1 0.0 copy-done.2
  581.1 0.0 copy-done.3
  581.1 0.8 copy-done.8
  581.8 0.0 copy-start.18
  581.8 0.0 copy-start.1
  581.8 0.0 copy-start.5
  581.8 0.0 copy-start.6
  581.9 0.0 copy-start.7
  581.9 4.4 fusion.9
  586.2 0.0 copy-done.18
  586.2 0.1 fusion.7
  586.3 0.0 copy-start.19
  586.4 0.1 broadcast_in_dim.12
  586.4 0.1 pad.2.clone
  586.5 0.1 maximum_maximum_fusion
  586.6 0.0 copy-done.1
  586.6 0.0 copy-done.5
  586.6 0.0 copy-done.6
  586.6 0.7 copy-done.7
  587.3 0.0 copy-start.4
  587.3 0.0 copy-start.10
  587.3 0.0 copy-start.11
  587.3 0.0 copy-start.12
  587.3 3.4 fusion.17
  590.7 0.0 copy-done.19
  590.7 0.0 copy-start.14
  590.7 0.0 copy-start.15
  590.7 0.0 copy-start.16
  590.7 0.0 copy-start.17
  590.7 0.0 copy-start.13
  590.7 0.0 copy-done.4
  590.7 0.0 copy-done.10
  590.8 0.0 copy-done.11
  590.8 0.0 copy-done.12
  590.8 0.0 copy-start.9
  590.8 1.5 fusion.15
  592.3 0.0 copy-done.14
  592.3 0.0 copy-done.15
  592.3 0.0 copy-done.16
  592.3 0.0 copy-done.17
  592.3 0.6 multiply_subtract_fusion.3
  592.9 0.0 copy-done.13
  592.9 0.8 copy.46
  593.7 0.0 copy-done.9
  593.7 1.0 copy.47
  (1 shorter events, 0.0 us)
Async XLA Ops:
  569.4 11.6 %copy-start = (f32[2048,256]{1,0:T(8,128)S(1)}, f32[2048,256]{1,0:T(8,128)}, u32[]{:S(2)}) copy-start(f32[2048,256]{1,0:T(8,128)} %refs_4_.1) | copy-start | bytes 6291460
  569.5 11.6 %copy-start.2 = (f32[2048,256]{1,0:T(8,128)S(1)}, f32[2048,256]{1,0:T(8,128)}, u32[]{:S(2)}) copy-start(f32[2048,256]{1,0:T(8,128)} %param.33) | copy-start | bytes 6291460
  569.5 11.6 %copy-start.3 = (f32[2048,256]{1,0:T(8,128)S(1)}, f32[2048,256]{1,0:T(8,128)}, u32[]{:S(2)}) copy-start(f32[2048,256]{1,0:T(8,128)} %param.34) | copy-start | bytes 6291460
  569.5 12.4 %copy-start.8 = (bf16[2048,256]{1,0:T(8,128)(2,1)S(1)}, bf16[2048,256]{1,0:T(8,128)(2,1)}, u32[]{:S(2)}) copy-start(bf16[2048,256]{1,0:T(8,128)(2,1)} %get-tuple-element.98) | copy-start | bytes 3145732
  581.8 4.4 copy-start.18
  581.8 4.8 copy-start.1
  581.8 4.8 copy-start.5
  581.8 4.8 copy-start.6
  581.9 5.4 copy-start.7
  586.3 4.4 copy-start.19
  587.3 3.4 copy-start.4
  587.3 3.4 copy-start.10
  587.3 3.5 copy-start.11
  587.3 3.5 copy-start.12
  590.7 1.6 copy-start.14
  590.7 1.6 copy-start.15
  590.7 1.6 copy-start.16
  590.7 1.6 copy-start.17
  590.7 2.2 copy-start.13
  590.8 2.9 copy-start.9
where the time goes:
time: 603 us; the launch traced here: 595 us
  Pallas kernels  567 us (94%)
  other arithmetic  21.6 us (4%)
    pallas_call x1, Pallas kernels, unit_kernel_call(): pl.pallas_call(kernel, out_shape=(shape((total_rows, width), bf16), shape...  230 us
    pallas_call x1, Pallas kernels, attend_back_call(): pl.pallas_call(kernel, out_shape=(shape((2, slab, outer * units), bf16),...  180 us
    pallas_call x1, Pallas kernels, open_call(): pl.pallas_call(kernel, out_shape=(shape((3, slab, units), bf16),) * parts...  157 us

commit v1 on v0

--- a/solution.py
+++ b/solution.py
@@ -106,15 +106,15 @@
     z_steps = list(range(1, outer))
 
     def kernel(*refs):
-        fixed, far_in, grads_in = refs[:17], refs[17:20], refs[20 : 20 + some]
-        rest = refs[20 + some :]
+        fixed, far_in, grads_in = refs[:16], refs[16:19], refs[19 : 19 + some]
+        rest = refs[19 + some :]
         body(*fixed, far_in, grads_in, *rest)
 
     def body(
         dres_ref, hat_ref, o_scale_ref, gain_ref, out_w, ctx, q_ref, k_ref, v_ref, lse_ref, scale_ref,
-        cos_ref, sin_ref, id_col, id_row, last_ref, tops_ref, far_in, grads_in,
+        cos_ref, sin_ref, id_row, last_ref, tops_ref, far_in, grads_in,
         gu_out, down_out, part_ref, part_out, gains_out, tops_out, tokens_out,
-        hats, seq, qkv_w, seq_do, d_ctx, d_q, d_k, d_v, d_low, probs_low, whole, terms, row_terms, turned,
+        hats, seq, qkv_w, seq_do, d_ctx, d_q, d_k, d_v, d_low, probs_low, id_col, whole, terms, row_terms, turned,
         land, land_gain, land_top, own_gain, peer_gain, inners, peer_inners,
         gu_land, gu_sum, down_land, down_sum, core_send, core_land, hold, chip_send, chip_land,
         s_ring, r_ring, s_row, r_row, s_in, r_in, s_y, r_y, s_z, r_z, s_core, r_core, s_chip, r_chip, s_gain, r_gain, local,
@@ -315,6 +315,7 @@
         for k in range(1, chips):
             moves.append(row_copy(k - 1, t_at, tensor_peer(k, 0)))
         to_core = row_copy(chips - 1, t_at, tensor_peer(0, 1))
+        id_col[...] = jnp.broadcast_to(id_row[...], (128, length)).T
         unit_sums(1)
         scale = HEAD ** (-0.5)
         for h in range(heads):
@@ -323,7 +324,7 @@
             def weigh(i, c, cols=cols, h=h):
                 at = rows_of(i, tall)
                 raw = dot(q_ref[at, cols], k_ref[:, cols], ((1,), (1,))) * scale
-                masked = jnp.where(id_row[...] <= id_col[at], raw, masked_value)
+                masked = jnp.where(id_row[...] <= id_col[at, 0:1], raw, masked_value)
                 probs_low[h, at] = jnp.exp(masked - lse_ref[at, h : h + 1]).astype(bf16)
                 return c
 
@@ -551,7 +552,7 @@
             shape(tops.shape, f32),
             shape((count, width), f32),
         ),
-        in_specs=[vmem] * 17 + [anywhere] * 3 + [anywhere] * some,
+        in_specs=[vmem] * 16 + [anywhere] * 3 + [anywhere] * some,
         out_specs=(anywhere,) * 2 + (vmem,) * 5,
         scratch_shapes=[
             pltpu.VMEM(hats.shape, f32),
@@ -564,6 +565,7 @@
             pltpu.VMEM((length, span), f32),
             pltpu.VMEM((3, length, span), bf16),
             pltpu.VMEM((heads, length, length), bf16),
+            pltpu.VMEM((length, 128), jnp.int32),
             pltpu.VMEM((4, span, width), bf16),
             pltpu.VMEM((n, 8, thin), f32),
             pltpu.VMEM((8, width), f32),
@@ -607,7 +609,7 @@
         ),
     )(
         d_resid, attn_hat, o_scale, gain_rows, full_out, context, q_low, k_low, v_low, lse, scales,
-        tables[0], tables[1], blocks[:, None], blocks[None, :], gain_last, tops,
+        tables[0], tables[1], blocks[None, :], gain_last, tops,
         hats, seq, full_qkv, *flat_grads,
     )
     return results
@@ -637,13 +639,13 @@
     mesh_id = pl.DeviceIdType.MESH
 
     def kernel(*refs):
-        body(*refs[:11], dict(zip(places, refs[11 : 11 + parts])), *refs[11 + parts :])
+        body(*refs[:10], dict(zip(places, refs[10 : 10 + parts])), *refs[10 + parts :])
 
     def body(
-        qkv_any, out_any, rows_any, gu_any, down_any, gains_ref, cos_ref, sin_ref, id_col, id_row, rows_ref,
+        qkv_any, out_any, rows_any, gu_any, down_any, gains_ref, cos_ref, sin_ref, id_row, rows_ref,
         pieces, qkv_out, flat_out, seq_out,
         gain_rows, hat_ref, scale_ref, q_low, k_low, v_low, lse_ref, context, attn_hat, o_scale, resid, resid_low, top_ref,
-        qkv_ref, out_w_ref, seq_ref, all_gains, qkv_wide, out_wide, gu_wide, down_wide, cast,
+        qkv_ref, out_w_ref, seq_ref, all_gains, qkv_wide, out_wide, gu_wide, down_wide, cast, id_col,
         square, squares, core_send, core_land, hold, chip_send, chip_land,
         s_ring, r_ring, s_row, r_row, s_z, r_z, s_y, r_y, s_sq, r_sq, s_core, r_core, s_chip, r_chip, local,
     ):
@@ -771,7 +773,10 @@
 
             looped(shard_units // 256, cast_rows)
 
-        shadows = [lambda: cast_wide(0), lambda: cast_wide(1), cast_turned]
+        def ids():
+            id_col[...] = jnp.broadcast_to(id_row[...], (128, length)).T
+
+        shadows = [ids, lambda: cast_wide(0), lambda: cast_wide(1), cast_turned]
         for step in range(1, n - 1):
             for item in order:
                 hops[step - 1, item].wait_recv()
@@ -886,7 +891,7 @@
             def attend(i, best, cols=cols, h=h):
                 at = rows_of(i, tall)
                 raw = dot(q_low[at, cols], k_low[:, cols], ((1,), (1,))) * scale
-                masked = jnp.where(id_row[...] <= id_col[at], raw, masked_value)
+                masked = jnp.where(id_row[...] <= id_col[at, 0:1], raw, masked_value)
                 top = jnp.max(masked, axis=1, keepdims=True)
                 weight = jnp.exp(masked - top)
                 total = jnp.sum(weight, axis=1, keepdims=True)
@@ -996,7 +1001,7 @@
             shape((count, width), bf16),
             shape((8, 128), f32),
         ),
-        in_specs=[anywhere] * 5 + [vmem] * 6,
+        in_specs=[anywhere] * 5 + [vmem] * 5,
         out_specs=(anywhere,) * (parts + 3) + (vmem,) * 13,
         scratch_shapes=[
             pltpu.VMEM((lead, width, span), bf16),
@@ -1008,6 +1013,7 @@
             pltpu.VMEM(w_gu.shape, f32),
             pltpu.VMEM(w_down.shape, f32),
             pltpu.VMEM((3, slab, shard_units), bf16),
+            pltpu.VMEM((length, 128), jnp.int32),
             pltpu.VMEM((8, length), f32),
             pltpu.VMEM((tensor - 1, 8, length), f32),
             pltpu.VMEM((chips, count, width), bf16),
@@ -1036,7 +1042,7 @@
         ),
     )(
         w_qkv, w_out, rows, w_gu, w_down, gains, tables[0], tables[1],
-        blocks[:, None], blocks[None, :], rows,
+        blocks[None, :], rows,
     )
     return dict(zip(places, results[:parts])), results[parts:]
 
@@ -1059,21 +1065,21 @@
     held = per if groups > 1 else max(per - 1, 1)
     links = outer * (chips - 1)
     steps = list(range(outer))
-    far_first = [0] + steps[2:] + steps[1:2]
+    near, far, rest = steps[1:2], steps[2:3], steps[3:]
 
     def units_of(of_steps):
         return [(s, i) for s in of_steps for i in range(groups)]
 
     orders = {
-        (0, 0): units_of(far_first),
-        (0, 1): units_of(far_first),
-        (1, 0): units_of(steps),
-        (1, 1): units_of(far_first),
+        (0, 0): units_of(far + [0] + rest + near),
+        (0, 1): units_of(far + rest + near + [0]),
+        (1, 0): units_of([0] + far + near + rest),
+        (1, 1): units_of([0] + far + near + rest),
     }
-    grad_order = units_of(far_first)
+    grad_order = units_of([0] + far + rest + near)
     tile = 512
     wide_tiles = width // tile
-    unit_tile = min(256, units)
+    unit_tile = min(512, units)
     lines = 32
     bf16, f32 = jnp.bfloat16, jnp.float32
     mesh_id = pl.DeviceIdType.MESH

time: 603 us -> 601 us (level)
  no operation moved by 1% of the time
where the time goes in v1:
time: 601 us; the launch traced here: 591 us
  Pallas kernels  565 us (94%)
  other arithmetic  21.5 us (4%)
    pallas_call x1, Pallas kernels, unit_kernel_call(): pl.pallas_call(kernel, out_shape=(shape((total_rows, width), bf16), shape...  225 us
    pallas_call x1, Pallas kernels, attend_back_call(): pl.pallas_call(kernel, out_shape=(shape((2, slab, outer * units), bf16),...  183 us
    pallas_call x1, Pallas kernels, open_call(): pl.pallas_call(kernel, out_shape=(shape((3, slab, units), bf16),) * parts...  157 us

profile of v1, /device:TPU:13, one launch (start us, length us, event | category | flops | bytes accessed | tf_op | source)
XLA Modules:
  0.0 590.9 jit_solution(2725447268220205132)
XLA Ops:
  0.7 157.3 %shard_map.363 = (bf16[3,256,512]{2,1,0:T(8,128)(2,1)}, bf16[3,256,512]{2,1,0:T(8,128)(2,1)}, bf16[3,256,512]{2,1,0:T(8,128)(2,1)}, bf16[3,256,512]{2,1,0:T(8,12...) custom-call(f32[3,256,512]{2,1,0:T(8,128)} %refs_0_.1, ...), custom_call_target="tpu_custom_call" | custom-call | tf_op jit(solution)/shard_map/pallas_call | solution.py:983
  158.0 225.1 %shard_map.364 = (bf16[128,2048]{1,0:T(8,128)(2,1)}, f32[128,2048]{1,0:T(8,128)}, f32[1,2048]{1,0:T(1,128)}, bf16[2,4,2,128,2048]{4,3,2,1,0:T(8,128)(2,1)}, bf16...) custom-call(bf16[3,256,512]{2,1,0:T(8,128)(2,1)} %get-tuple-element., ...), custom_call_target="tpu_custom_call" | custom-call | flops 38654705664 | bytes 67108864 | tf_op jit(solution)/shard_map/pallas_call | solution.py:1602
  383.0 182.6 %shard_map.365 = (bf16[2,256,2048]{2,1,0:T(8,128)(2,1)}, bf16[2048,256]{1,0:T(8,128)(2,1)}, f32[3,256,512]{2,1,0:T(8,128)}, f32[512,256]{1,0:T(8,128)}, f32[8,25...) custom-call(f32[128,2048]{1,0:T(8,128)} %get-tuple-element.72.refs_0_, f32[128,2048]{1,0:T(8,128)} %get-tuple-element.73.refs_1_, ...), custom_call_target="tpu_custom_call" | custom-call | tf_op jit(solution)/shard_map/pallas_call | solution.py:544
  565.6 0.0 copy-start
  565.7 0.0 copy-start.2
  565.7 0.0 copy-start.3
  565.7 0.0 copy-start.8
  565.7 11.4 %fusion.12 = (bf16[2,256,2048]{2,1,0:T(8,128)(2,1)}, f32[2,256,2048]{2,1,0:T(8,128)}, f32[2,256,2048]{2,1,0:T(8,128)}, f32[2,256,2048]{2,1,0:T(8,128)}) fusion(f32[2,256,2048]{2,1,0:T(8,128)} %refs_3_.1, bf16[2,256,2048]{2,1,0:T(8,128)(2,1)} %get-tuple-element.97, f32[2,256,2048]{2,1,0:T(8,128)} %param.30, f32[2,256,2048]{2,1,0:T(8,128)} %param.31), kind=kLoop, calls=%fused_computation.26 | loop fusion | flops 17825792 | bytes 29360128 | tf_op jit(solution)/shard_map/convert_element_type | solution.py:1774
  577.1 0.0 copy-done
  577.1 0.0 copy-done.2
  577.1 0.0 copy-done.3
  577.1 0.5 copy-done.8
  577.6 0.0 copy-start.18
  577.6 0.0 copy-start.1
  577.6 0.0 copy-start.5
  577.6 0.0 copy-start.6
  577.6 0.0 copy-start.7
  577.6 4.4 fusion.9
  582.0 0.0 copy-done.18
  582.0 0.1 fusion.7
  582.1 0.0 copy-start.19
  582.1 0.1 broadcast_in_dim.12
  582.2 0.1 pad.2.clone
  582.3 0.1 maximum_maximum_fusion
  582.3 0.0 copy-done.1
  582.3 0.0 copy-done.5
  582.3 0.0 copy-done.6
  582.3 0.7 copy-done.7
  583.0 0.0 copy-start.4
  583.0 0.0 copy-start.10
  583.0 0.0 copy-start.11
  583.0 0.0 copy-start.12
  583.1 3.4 fusion.17
  586.4 0.0 copy-done.19
  586.4 0.0 copy-start.14
  586.4 0.0 copy-start.15
  586.5 0.0 copy-start.16
  586.5 0.0 copy-start.17
  586.5 0.0 copy-start.13
  586.5 0.0 copy-done.4
  586.5 0.0 copy-done.10
  586.5 0.0 copy-done.11
  586.5 0.0 copy-done.12
  586.5 0.0 copy-start.9
  586.5 1.5 fusion.15
  588.0 0.0 copy-done.14
  588.0 0.0 copy-done.15
  588.0 0.0 copy-done.16
  588.0 0.0 copy-done.17
  588.0 0.6 multiply_subtract_fusion.3
  588.7 0.0 copy-done.13
  588.7 0.8 copy.44
  589.5 0.0 copy-done.9
  589.5 1.0 copy.45
  (1 shorter events, 0.0 us)
Async XLA Ops:
  565.6 11.4 %copy-start = (f32[2048,256]{1,0:T(8,128)S(1)}, f32[2048,256]{1,0:T(8,128)}, u32[]{:S(2)}) copy-start(f32[2048,256]{1,0:T(8,128)} %refs_4_.1) | copy-start | bytes 6291460
  565.7 11.4 %copy-start.2 = (f32[2048,256]{1,0:T(8,128)S(1)}, f32[2048,256]{1,0:T(8,128)}, u32[]{:S(2)}) copy-start(f32[2048,256]{1,0:T(8,128)} %param.33) | copy-start | bytes 6291460
  565.7 11.4 %copy-start.3 = (f32[2048,256]{1,0:T(8,128)S(1)}, f32[2048,256]{1,0:T(8,128)}, u32[]{:S(2)}) copy-start(f32[2048,256]{1,0:T(8,128)} %param.34) | copy-start | bytes 6291460
  565.7 11.9 %copy-start.8 = (bf16[2048,256]{1,0:T(8,128)(2,1)S(1)}, bf16[2048,256]{1,0:T(8,128)(2,1)}, u32[]{:S(2)}) copy-start(bf16[2048,256]{1,0:T(8,128)(2,1)} %get-tuple-element.98) | copy-start | bytes 3145732
  577.6 4.4 copy-start.18
  577.6 4.8 copy-start.1
  577.6 4.8 copy-start.5
  577.6 4.8 copy-start.6
  577.6 5.4 copy-start.7
  582.1 4.4 copy-start.19
  583.0 3.4 copy-start.4
  583.0 3.4 copy-start.10
  583.0 3.5 copy-start.11
  583.0 3.5 copy-start.12
  586.4 1.6 copy-start.14
  586.4 1.6 copy-start.15
  586.5 1.6 copy-start.16
  586.5 1.6 copy-start.17
  586.5 2.2 copy-start.13
  586.5 2.9 copy-start.9

commit v2 on v1

--- a/solution.py
+++ b/solution.py
@@ -115,7 +115,7 @@
         cos_ref, sin_ref, id_row, last_ref, tops_ref, far_in, grads_in,
         gu_out, down_out, part_ref, part_out, gains_out, tops_out, tokens_out,
         hats, seq, qkv_w, seq_do, d_ctx, d_q, d_k, d_v, d_low, probs_low, id_col, whole, terms, row_terms, turned,
-        land, land_gain, land_top, own_gain, peer_gain, inners, peer_inners,
+        land, land_gain, land_top, peer_terms, inners, peer_inners,
         gu_land, gu_sum, down_land, down_sum, core_send, core_land, hold, chip_send, chip_land,
         s_ring, r_ring, s_row, r_row, s_in, r_in, s_y, r_y, s_z, r_z, s_core, r_core, s_chip, r_chip, s_gain, r_gain, local,
     ):
@@ -268,7 +268,7 @@
                     here[...] = summed.astype(here.dtype)
                     hop(step, item)
                 elif item == gain_item:
-                    own_gain[0] = summed
+                    gains_out[...] = summed
                 elif item == top_item:
                     tops_out[...] = summed
                 else:
@@ -301,9 +301,9 @@
             return total + jnp.sum(value * hat, axis=0, keepdims=True)
 
         gain_attn = lax.fori_loop(0, count // lines, open_rows, jnp.zeros((1, width), f32))
-        row_terms[...] = jnp.zeros((8, width), f32)
-        row_terms[2:3] = gain_attn
-        row_terms[3:4] = last_ref[...]
+        row_terms[0] = jnp.zeros((8, width), f32)
+        row_terms[0, 2:3] = gain_attn
+        row_terms[0, 3:4] = last_ref[...]
         moves, passed = [], []
 
         def row_copy(slot, index, peer):
@@ -399,8 +399,8 @@
         zero = jnp.zeros((1, span), f32)
         gain_q, gain_k = lax.fori_loop(0, length // tall, unrotate, (zero, zero))
         offset = rows_of(t_at, span)
-        row_terms[0:1, offset] = gain_q
-        row_terms[1:2, offset] = gain_k
+        row_terms[0, 0:1, offset] = gain_q
+        row_terms[0, 1:2, offset] = gain_k
         in_copies = []
         for k in range(chips):
             for f in (0, 1):
@@ -410,10 +410,17 @@
                         remote(inners, peer_inners.at[at], s_in.at[at], r_in.at[at], tensor_peer(k, f))
                     )
         sent.extend(in_copies)
+        first = remote(row_terms.at[0], peer_terms.at[0], s_gain.at[0], r_gain.at[0], tensor_peer(0, 1))
         matrix_grad(3, ctx[...], seq_do)
         depart(3, 7)
         for copy in in_copies:
             copy.wait_recv()
+        first.wait_recv()
+        row_terms[1] = row_terms[0] + peer_terms[0]
+        others = [
+            remote(row_terms.at[1], peer_terms.at[k], s_gain.at[k], r_gain.at[k], tensor_peer(k, 0))
+            for k in range(1, chips)
+        ]
         unit_sums(1)
 
         def normed(i):
@@ -434,9 +441,15 @@
             depart(c, c + 4)
             unit_sums(1)
 
+        for copy in others:
+            copy.wait_recv()
+
         def place_terms(i, c):
             cols = pl.ds(pl.multiple_of(i * thin, thin), thin)
-            terms[i] = row_terms[:, cols]
+            total = row_terms[1, :, cols]
+            for k in range(1, chips):
+                total = total + peer_terms[k, :, cols]
+            terms[i] = total
             return c
 
         lax.fori_loop(0, n, place_terms, 0)
@@ -515,19 +528,6 @@
             for _ in range(per_step):
                 if duties:
                     duties.pop(0)()
-        peers = [tensor_peer(0, 1)] + [tensor_peer(k, 0) for k in range(1, chips)]
-        first = remote(own_gain.at[0], peer_gain.at[0], s_gain.at[0], r_gain.at[0], peers[0])
-        first.wait_recv()
-        own_gain[1] = own_gain[0] + peer_gain[0]
-        others = [
-            remote(own_gain.at[1], peer_gain.at[k], s_gain.at[k], r_gain.at[k], peers[k])
-            for k in range(1, chips)
-        ]
-        result = own_gain[1]
-        for k in range(1, chips):
-            others[k - 1].wait_recv()
-            result = result + peer_gain[k]
-        gains_out[...] = result
         for copy in z_copies:
             copy.wait()
         for copy in keeps:
@@ -568,13 +568,12 @@
             pltpu.VMEM((length, 128), jnp.int32),
             pltpu.VMEM((4, span, width), bf16),
             pltpu.VMEM((n, 8, thin), f32),
-            pltpu.VMEM((8, width), f32),
+            pltpu.VMEM((2, 8, width), f32),
             pltpu.VMEM((span, length), bf16),
             pltpu.VMEM((n - 1, 8, half, thin), bf16),
             pltpu.VMEM((n - 1, 8, thin), f32),
             pltpu.VMEM((n - 1,) + tops.shape, f32),
-            pltpu.VMEM((2, 8, thin), f32),
-            pltpu.VMEM((chips, 8, thin), f32),
+            pltpu.VMEM((chips, 8, width), f32),
             pltpu.VMEM((8, length), f32),
             pltpu.VMEM((tensor - 1, 8, length), f32),
             pltpu.VMEM((max(inner - 1, 1), 2, outer, slab, units), bf16),
@@ -1065,21 +1064,21 @@
     held = per if groups > 1 else max(per - 1, 1)
     links = outer * (chips - 1)
     steps = list(range(outer))
-    near, far, rest = steps[1:2], steps[2:3], steps[3:]
+    far_first = [0] + steps[2:] + steps[1:2]
 
     def units_of(of_steps):
         return [(s, i) for s in of_steps for i in range(groups)]
 
     orders = {
-        (0, 0): units_of(far + [0] + rest + near),
-        (0, 1): units_of(far + rest + near + [0]),
-        (1, 0): units_of([0] + far + near + rest),
-        (1, 1): units_of([0] + far + near + rest),
+        (0, 0): units_of(far_first),
+        (0, 1): units_of(far_first),
+        (1, 0): units_of(steps),
+        (1, 1): units_of(far_first),
     }
-    grad_order = units_of([0] + far + rest + near)
+    grad_order = units_of(far_first)
     tile = 512
     wide_tiles = width // tile
-    unit_tile = min(512, units)
+    unit_tile = min(256, units)
     lines = 32
     bf16, f32 = jnp.bfloat16, jnp.float32
     mesh_id = pl.DeviceIdType.MESH

time: 601 us -> 599 us (level)
    pallas_call x1, Pallas kernels: 183 us -> 176 us  [attend_back_call(): pl.pallas_call(kernel, out_shape=(shape((2, slab, outer * units), bf16),...]
where the time goes in v2:
time: 599 us; the launch traced here: 590 us
  Pallas kernels  564 us (94%)
  other arithmetic  21.6 us (4%)
    pallas_call x1, Pallas kernels, unit_kernel_call(): pl.pallas_call(kernel, out_shape=(shape((total_rows, width), bf16), shape...  230 us
    pallas_call x1, Pallas kernels, attend_back_call(): pl.pallas_call(kernel, out_shape=(shape((2, slab, outer * units), bf16),...  176 us
    pallas_call x1, Pallas kernels, open_call(): pl.pallas_call(kernel, out_shape=(shape((3, slab, units), bf16),) * parts...  157 us

profile of v2, /device:TPU:13, one launch (start us, length us, event | category | flops | bytes accessed | tf_op | source)
XLA Modules:
  0.0 589.9 jit_solution(15178842673822139670)
XLA Ops:
  0.7 157.3 %shard_map.363 = (bf16[3,256,512]{2,1,0:T(8,128)(2,1)}, bf16[3,256,512]{2,1,0:T(8,128)(2,1)}, bf16[3,256,512]{2,1,0:T(8,128)(2,1)}, bf16[3,256,512]{2,1,0:T(8,12...) custom-call(f32[3,256,512]{2,1,0:T(8,128)} %refs_0_.1, ...), custom_call_target="tpu_custom_call" | custom-call | tf_op jit(solution)/shard_map/pallas_call | solution.py:982
  158.0 230.0 %shard_map.364 = (bf16[128,2048]{1,0:T(8,128)(2,1)}, f32[128,2048]{1,0:T(8,128)}, f32[1,2048]{1,0:T(1,128)}, bf16[2,4,2,128,2048]{4,3,2,1,0:T(8,128)(2,1)}, bf16...) custom-call(bf16[3,256,512]{2,1,0:T(8,128)(2,1)} %get-tuple-element., ...), custom_call_target="tpu_custom_call" | custom-call | flops 38654705664 | bytes 67108864 | tf_op jit(solution)/shard_map/pallas_call | solution.py:1601
  388.0 176.4 %shard_map.365 = (bf16[2,256,2048]{2,1,0:T(8,128)(2,1)}, bf16[2048,256]{1,0:T(8,128)(2,1)}, f32[3,256,512]{2,1,0:T(8,128)}, f32[512,256]{1,0:T(8,128)}, f32[8,25...) custom-call(f32[128,2048]{1,0:T(8,128)} %get-tuple-element.72.refs_0_, f32[128,2048]{1,0:T(8,128)} %get-tuple-element.73.refs_1_, ...), custom_call_target="tpu_custom_call" | custom-call | tf_op jit(solution)/shard_map/pallas_call | solution.py:544
  564.4 0.0 copy-start
  564.5 0.0 copy-start.2
  564.5 0.0 copy-start.3
  564.5 0.0 copy-start.8
  564.5 11.6 %fusion.12 = (bf16[2,256,2048]{2,1,0:T(8,128)(2,1)}, f32[2,256,2048]{2,1,0:T(8,128)}, f32[2,256,2048]{2,1,0:T(8,128)}, f32[2,256,2048]{2,1,0:T(8,128)}) fusion(f32[2,256,2048]{2,1,0:T(8,128)} %refs_3_.1, bf16[2,256,2048]{2,1,0:T(8,128)(2,1)} %get-tuple-element.97, f32[2,256,2048]{2,1,0:T(8,128)} %param.30, f32[2,256,2048]{2,1,0:T(8,128)} %param.31), kind=kLoop, calls=%fused_computation.26 | loop fusion | flops 17825792 | bytes 29360128 | tf_op jit(solution)/shard_map/convert_element_type | solution.py:1773
  576.1 0.0 copy-done
  576.1 0.0 copy-done.2
  576.1 0.0 copy-done.3
  576.1 0.8 copy-done.8
  576.8 0.0 copy-start.18
  576.8 0.0 copy-start.1
  576.9 0.0 copy-start.5
  576.9 0.0 copy-start.6
  576.9 0.0 copy-start.7
  576.9 4.4 fusion.9
  581.2 0.0 copy-done.18
  581.2 0.1 fusion.7
  581.4 0.0 copy-start.19
  581.4 0.1 broadcast_in_dim.12
  581.4 0.1 pad.2.clone
  581.5 0.1 maximum_maximum_fusion
  581.6 0.0 copy-done.1
  581.6 0.0 copy-done.5
  581.6 0.0 copy-done.6
  581.6 0.7 copy-done.7
  582.3 0.0 copy-start.4
  582.3 0.0 copy-start.10
  582.3 0.0 copy-start.11
  582.3 0.0 copy-start.12
  582.3 3.4 fusion.17
  585.7 0.0 copy-done.19
  585.7 0.0 copy-start.14
  585.7 0.0 copy-start.15
  585.7 0.0 copy-start.16
  585.7 0.0 copy-start.17
  585.7 0.0 copy-start.13
  585.7 0.0 copy-done.4
  585.8 0.0 copy-done.10
  585.8 0.0 copy-done.11
  585.8 0.0 copy-done.12
  585.8 0.0 copy-start.9
  585.8 1.5 fusion.15
  587.3 0.0 copy-done.14
  587.3 0.0 copy-done.15
  587.3 0.0 copy-done.16
  587.3 0.0 copy-done.17
  587.3 0.6 multiply_subtract_fusion.3
  587.9 0.0 copy-done.13
  587.9 0.8 copy.44
  588.7 0.0 copy-done.9
  588.7 1.0 copy.45
  (1 shorter events, 0.0 us)
Async XLA Ops:
  564.4 11.6 %copy-start = (f32[2048,256]{1,0:T(8,128)S(1)}, f32[2048,256]{1,0:T(8,128)}, u32[]{:S(2)}) copy-start(f32[2048,256]{1,0:T(8,128)} %refs_4_.1) | copy-start | bytes 6291460
  564.5 11.6 %copy-start.2 = (f32[2048,256]{1,0:T(8,128)S(1)}, f32[2048,256]{1,0:T(8,128)}, u32[]{:S(2)}) copy-start(f32[2048,256]{1,0:T(8,128)} %param.33) | copy-start | bytes 6291460
  564.5 11.6 %copy-start.3 = (f32[2048,256]{1,0:T(8,128)S(1)}, f32[2048,256]{1,0:T(8,128)}, u32[]{:S(2)}) copy-start(f32[2048,256]{1,0:T(8,128)} %param.34) | copy-start | bytes 6291460
  564.5 12.4 %copy-start.8 = (bf16[2048,256]{1,0:T(8,128)(2,1)S(1)}, bf16[2048,256]{1,0:T(8,128)(2,1)}, u32[]{:S(2)}) copy-start(bf16[2048,256]{1,0:T(8,128)(2,1)} %get-tuple-element.98) | copy-start | bytes 3145732
  576.8 4.4 copy-start.18
  576.8 4.8 copy-start.1
  576.9 4.8 copy-start.5
  576.9 4.8 copy-start.6
  576.9 5.4 copy-start.7
  581.4 4.4 copy-start.19
  582.3 3.4 copy-start.4
  582.3 3.4 copy-start.10
  582.3 3.5 copy-start.11
  582.3 3.5 copy-start.12
  585.7 1.6 copy-start.14
  585.7 1.6 copy-start.15
  585.7 1.6 copy-start.16
  585.7 1.6 copy-start.17
  585.7 2.2 copy-start.13
  585.8 2.9 copy-start.9
